TPU v7x, 32 devices: a whole 2x2x4 slice. The times are simulated.
32 devices in a mesh: gx: 4 (over x, core), gy: 8 (over z, y).
Axes of the slice: x: 2, y: 2, z: 4, core: 2. Of those that a mesh axis runs over, the one named last changes fastest.
Arguments:
- flux: float32 [8, 256, 2048], P(None, 'gx', 'gy'), may hold values from -6 to 6
- diffusivity: float32 [128, 1024], P('gx', 'gy'), may hold values from 0.08 to 0.24
- remap_bank: bfloat16 [16, 3, 256, 128], replicated, may hold values from -0.21875 to 0.21875
- rec_owner: int32 [4096], P(('gx', 'gy')), may hold values from 0 to 31, as said below
- rec_source: int32 [4096], P(('gx', 'gy')), may hold values from 0 to 63
- rec_target: int32 [4096], P(('gx', 'gy')), may hold values from 0 to 31
- rec_weight: int32 [4096], P(('gx', 'gy')), may hold values from 0 to 15
Outputs:
- ocean_state: float32 [8, 128, 1024], P(None, 'gx', 'gy')
Inputs may be any that keep to these rules, and one draw needn't show every extreme that they name: `rec_owner`: among the records of one atmosphere block each owner appears at most 8 times; in every draw some owner appears exactly 8 times in every block's records.
All inputs are finite; a program needn't handle non-finite values.
Results may differ from a plain program's by a relative error of at most 0.0029.
Values may be sent and summed in bfloat16 or wider, within the bound.
A program may use at most 64 MiB of HBM per device.

v0:
```python
import math

import jax
import jax.numpy as jnp
from jax import lax
from jax.sharding import PartitionSpec as P

TILE_X = 16
TILE_Y = 16
OTILE_X = 8
OTILE_Y = 16
SWEEPS = 4


def extended(cells, sides, width, closed):
    for axis, dim in sides:
        count = lax.axis_size(axis)
        ends = count if closed else count - 1
        head = lax.slice_in_dim(cells, 0, width, axis=dim)
        tail = lax.slice_in_dim(cells, cells.shape[dim] - width, cells.shape[dim], axis=dim)
        cells = jnp.concatenate(
            [
                lax.ppermute(tail, axis, [(i, (i + 1) % count) for i in range(ends)]),
                cells,
                lax.ppermute(head, axis, [((i + 1) % count, i) for i in range(ends)]),
            ],
            axis=dim,
        )
    return cells


def block_products(source_part, weight_ids, remap_bank):
    bank_part = remap_bank[jnp.maximum(weight_ids, 0)]
    return jnp.einsum("gkfc,gkco->gfo", source_part, bank_part, preferred_element_type=jnp.float32)


def record_products(picked, weight_ids, remap_bank):
    records = picked.shape[0]
    group_size = math.gcd(records, 32)
    block_count = records // group_size

    def one_block(carry, pieces):
        return (carry, block_products(pieces[0], pieces[1], remap_bank))

    unused, stacked = lax.scan(
        one_block,
        0,
        (
            picked.reshape((block_count, group_size) + picked.shape[1:]),
            weight_ids.reshape(block_count, group_size),
        ),
    )
    return stacked.reshape((records,) + stacked.shape[2:])


def ocean_grid(forcing, grid_rows, grid_cols):
    fields = forcing.shape[1]
    tiles_x = grid_rows // OTILE_X
    tiles_y = grid_cols // OTILE_Y
    shaped = forcing.reshape(tiles_x, tiles_y, fields, OTILE_X, OTILE_Y)
    return shaped.transpose(2, 0, 3, 1, 4).reshape(fields, grid_rows, grid_cols)


def local(flux, diffusivity, remap_bank, rec_owner, rec_source, rec_target, rec_weight):
    fields, grid_rows, grid_cols = flux.shape
    padded = extended(flux, (("gx", 1), ("gy", 2)), 1, True)
    slope_x = (padded[:, 2:, 1:-1] - padded[:, :-2, 1:-1]) * 0.5
    slope_y = (padded[:, 1:-1, 2:] - padded[:, 1:-1, :-2]) * 0.5
    coeffs = jnp.stack([flux, slope_x, slope_y]).astype(jnp.bfloat16)
    tile_cells = TILE_X * TILE_Y
    source_tiles = coeffs.reshape(
        3, fields, grid_rows // TILE_X, TILE_X, grid_cols // TILE_Y, TILE_Y
    )
    source_tiles = source_tiles.transpose(2, 4, 0, 1, 3, 5).reshape(-1, 3, fields, tile_cells)
    owners = lax.axis_size(("gx", "gy"))
    records = rec_owner.shape[0]
    capacity = max(2, 2 * records // owners)
    slot_count = owners * capacity
    owner_ids = jnp.arange(owners, dtype=jnp.int32)
    member = (rec_owner[:, None] == owner_ids[None, :]).astype(jnp.int32)
    before = jnp.cumsum(member, axis=0) - member
    slot_rank = jnp.sum(before * member, axis=1)
    slot_of = rec_owner * capacity + slot_rank
    ocean_rows, ocean_cols = diffusivity.shape
    tile_total = ocean_rows // OTILE_X * (ocean_cols // OTILE_Y)
    tile_ids = jnp.arange(tile_total, dtype=jnp.int32)
    picked = source_tiles[rec_source]
    partial_value = record_products(picked, rec_weight, remap_bank)
    outgoing = (
        jnp.zeros((slot_count,) + partial_value.shape[1:], jnp.float32)
        .at[slot_of]
        .set(partial_value)
    )
    aimed_tile = jnp.full((slot_count,), -1, jnp.int32).at[slot_of].set(rec_target)
    arrived, arrived_tile = (
        lax.all_to_all(outgoing, ("gx", "gy"), split_axis=0, concat_axis=0, tiled=True),
        lax.all_to_all(aimed_tile, ("gx", "gy"), split_axis=0, concat_axis=0, tiled=True),
    )
    onehot = (arrived_tile[:, None] == tile_ids[None, :]).astype(jnp.float32)
    forcing = jnp.einsum("st,sfo->tfo", onehot, arrived, precision=lax.Precision.HIGHEST)
    ocean = ocean_grid(forcing, ocean_rows, ocean_cols)
    for sweep in range(SWEEPS):
        bordered = extended(ocean, (("gx", 1), ("gy", 2)), 1, False)
        beside_all = (
            bordered[:, 2:, 1:-1]
            + bordered[:, :-2, 1:-1]
            + bordered[:, 1:-1, 2:]
            + bordered[:, 1:-1, :-2]
        )
        ocean = ocean + diffusivity * (beside_all - 4.0 * ocean)
    return ocean


def solution(mesh):
    in_specs = (
        P(None, "gx", "gy"),
        P("gx", "gy"),
        P(),
        P(("gx", "gy")),
        P(("gx", "gy")),
        P(("gx", "gy")),
        P(("gx", "gy")),
    )
    out_specs = P(None, "gx", "gy")
    return jax.shard_map(local, mesh=mesh, in_specs=in_specs, out_specs=out_specs, check_vma=False)
```

profile of v0, /device:TPU:0, one launch (start us, length us, event | category | flops | bytes accessed | tf_op | source)
XLA Modules:
  0.0 217.8 jit_solution(3283264019500223906)
XLA Ops:
  7.5 6.1 %all-to-all-start = ((s32[32,8,1]{1,2,0:T(1,128)}), s32[32,8,1]{1,2,0:T(1,128)S(1)}, u32[]{:S(2)}, u32[]{:S(2)}) async-start(s32[32,8,1]{1,2,0:T(1,128)} %bitcast.5), calls=%async_computation | async-start | bytes 32768 | tf_op jit(solution)/shard_map/all_to_all | solution.py:97
  15.6 4.6 %collective-permute-start.2 = (f32[8,66,1]{2,1,0:T(8,128)S(1)}, f32[8,66,1]{2,1,0:T(8,128)S(1)}, u32[]{:S(2)}, u32[]{:S(2)}) collective-permute-start(f32[8,66,1]{2,1,0:T(8,128)S(1)} %get-tuple-element.43), channel_id=1, source_target_pairs={{1,0},{2,1},{3,2},{4,3},{5,4},{6,5},{7,6},{0,7},{9,8},{10,9},{11,1... | collective-permute-start | bytes 6344 | tf_op jit(solution)/shard_map/ppermute | solution.py:25
  20.9 5.8 %collective-permute-done.2 = f32[8,66,1]{2,1,0:T(8,128)S(1)} collective-permute-done((f32[8,66,1]{2,1,0:T(8,128)S(1)}, f32[8,66,1]{2,1,0:T(8,128)S(1)}, u32[]{:S(2)}, u32[]{:S(2)}) %collective-permute-start.2) | collective-permute-done | bytes 2144 | tf_op jit(solution)/shard_map/ppermute | solution.py:25
  26.8 4.9 %collective-permute-done.3 = f32[8,66,1]{2,1,0:T(8,128)S(1)} collective-permute-done((f32[8,66,1]{2,1,0:T(8,128)S(1)}, f32[8,66,1]{2,1,0:T(8,128)S(1)}, u32[]{:S(2)}, u32[]{:S(2)}) %collective-permute-start.3) | collective-permute-done | bytes 2144 | tf_op jit(solution)/shard_map/ppermute | solution.py:23
  44.6 4.0 %maximum_bitcast_fusion = bf16[4,16,3,8,16,16]{5,4,3,2,1,0:T(8,128)(2,1)} fusion(bf16[1,8,4,16,16,16]{5,3,1,0,4,2:T(8,128)(2,1)S(1)} %copy.18, bf16[1,8,4,16,16,16]{5,3,1,0,4,2:T(8,128)(2,1)S(1)} %copy-done.2, bf16[1,8,4,16,16,16]{5,3,1,0,4,2:T(8,128)(2,1)S(1)} %copy-done.1), kind=kLoop, calls=%fused_computation.13 | loop fusion | flops 786432 | bytes 1572864 | tf_op jit(solution)/shard_map/transpose | solution.py:74
  48.6 8.6 %reshape.46 = bf16[64,3,8,256]{3,2,1,0:T(8,128)(2,1)} reshape(bf16[4,16,3,8,16,16]{5,4,3,2,1,0:T(8,128)(2,1)} %maximum_bitcast_fusion) | data formatting | bytes 1572864 | tf_op jit(solution)/shard_map/reshape | solution.py:74
  57.2 3.1 %gather_fusion.1 = bf16[128,3,8,256]{3,2,1,0:T(8,128)(2,1)} fusion(bf16[64,3,8,256]{3,2,1,0:T(8,128)(2,1)} %reshape.46, s32[1024]{0:T(1024)S(1)} %pad_clamp_fusion.1), kind=kCustom, calls=%fused_computation.1 | custom fusion | bytes 3146240 | tf_op jit(solution)/shard_map/gather | solution.py:87
  60.3 34.1 %while.10 = (s32[]{:T(128)}, f32[4,32,8,128]{3,2,1,0:T(8,128)}, bf16[4,32,3,8,256]{4,3,2,1,0:T(8,128)(2,1)}, s32[4,32]{1,0:T(4,128)S(1)}, bf16[16,3,256,128]{3,2,1,0:T(8,128)(2,1)S(1)}, /*index=5*/s32[]{:T(128)}) while((s32[]{:T(128)}, f32[4,32,8,128]{3,2,1,0:T(8,128)}, bf16[4,32,3,8,256]{4,3,2,1,0:T(8,128)(2,1)}, s32[4,32]{1,0:T(4,128)S(1)}, ...), condition=%wide.region_4.5_spmd, body=%wide.region_3.4_spmd.sunk | while | flops 50332704 | bytes 19404360 | solution.py:45
  60.3 4.0 %gather_fusion = bf16[32,3,256,128]{3,2,1,0:T(8,128)(2,1)} fusion(bf16[16,3,256,128]{3,2,1,0:T(8,128)(2,1)S(1)} %get-tuple-element.113, s32[1024]{0:T(1024)S(1)} %pad_clamp_fusion.3), kind=kCustom, calls=%fused_computation.clone.1 | custom fusion | bytes 12583040 | tf_op jit(solution)/shard_map/while/body/eval_jaxpr/gather | solution.py:33
  64.3 4.5 %fusion.62 = f32[4,32,8,128]{3,2,1,0:T(8,128)} fusion(f32[4,32,8,128]{3,2,1,0:T(8,128)} %get-tuple-element.104, s32[]{:T(128)} %get-tuple-element.103, bf16[32,3,256,128]{3,2,1,0:T(8,128)(2,1)} %gather_fusion, bf16[4,32,3,8,256]{4,3,2,1,0:T(8,128)(2,1)} %get-tuple-element.111), kind=kOutput, calls=%fused_computation.5.clone.1 | convolution fusion | flops 50331648 | bytes 6816768 | tf_op jit(solution)/shard_map/while/body/eval_jaxpr/gkfc,gkco->gfo/dot_general | solution.py:34
  68.8 4.0 %gather_fusion = bf16[32,3,256,128]{3,2,1,0:T(8,128)(2,1)} fusion(bf16[16,3,256,128]{3,2,1,0:T(8,128)(2,1)S(1)} %get-tuple-element.113, s32[1024]{0:T(1024)S(1)} %pad_clamp_fusion.3), kind=kCustom, calls=%fused_computation.clone.1 | custom fusion | bytes 12583040 | tf_op jit(solution)/shard_map/while/body/eval_jaxpr/gather | solution.py:33
  72.9 4.5 %fusion.62 = f32[4,32,8,128]{3,2,1,0:T(8,128)} fusion(f32[4,32,8,128]{3,2,1,0:T(8,128)} %get-tuple-element.104, s32[]{:T(128)} %get-tuple-element.103, bf16[32,3,256,128]{3,2,1,0:T(8,128)(2,1)} %gather_fusion, bf16[4,32,3,8,256]{4,3,2,1,0:T(8,128)(2,1)} %get-tuple-element.111), kind=kOutput, calls=%fused_computation.5.clone.1 | convolution fusion | flops 50331648 | bytes 6816768 | tf_op jit(solution)/shard_map/while/body/eval_jaxpr/gkfc,gkco->gfo/dot_general | solution.py:34
  77.4 4.0 %gather_fusion = bf16[32,3,256,128]{3,2,1,0:T(8,128)(2,1)} fusion(bf16[16,3,256,128]{3,2,1,0:T(8,128)(2,1)S(1)} %get-tuple-element.113, s32[1024]{0:T(1024)S(1)} %pad_clamp_fusion.3), kind=kCustom, calls=%fused_computation.clone.1 | custom fusion | bytes 12583040 | tf_op jit(solution)/shard_map/while/body/eval_jaxpr/gather | solution.py:33
  81.4 4.5 %fusion.62 = f32[4,32,8,128]{3,2,1,0:T(8,128)} fusion(f32[4,32,8,128]{3,2,1,0:T(8,128)} %get-tuple-element.104, s32[]{:T(128)} %get-tuple-element.103, bf16[32,3,256,128]{3,2,1,0:T(8,128)(2,1)} %gather_fusion, bf16[4,32,3,8,256]{4,3,2,1,0:T(8,128)(2,1)} %get-tuple-element.111), kind=kOutput, calls=%fused_computation.5.clone.1 | convolution fusion | flops 50331648 | bytes 6816768 | tf_op jit(solution)/shard_map/while/body/eval_jaxpr/gkfc,gkco->gfo/dot_general | solution.py:34
  85.9 4.0 %gather_fusion = bf16[32,3,256,128]{3,2,1,0:T(8,128)(2,1)} fusion(bf16[16,3,256,128]{3,2,1,0:T(8,128)(2,1)S(1)} %get-tuple-element.113, s32[1024]{0:T(1024)S(1)} %pad_clamp_fusion.3), kind=kCustom, calls=%fused_computation.clone.1 | custom fusion | bytes 12583040 | tf_op jit(solution)/shard_map/while/body/eval_jaxpr/gather | solution.py:33
  89.9 4.5 %fusion.62 = f32[4,32,8,128]{3,2,1,0:T(8,128)} fusion(f32[4,32,8,128]{3,2,1,0:T(8,128)} %get-tuple-element.104, s32[]{:T(128)} %get-tuple-element.103, bf16[32,3,256,128]{3,2,1,0:T(8,128)(2,1)} %gather_fusion, bf16[4,32,3,8,256]{4,3,2,1,0:T(8,128)(2,1)} %get-tuple-element.111), kind=kOutput, calls=%fused_computation.5.clone.1 | convolution fusion | flops 50331648 | bytes 6816768 | tf_op jit(solution)/shard_map/while/body/eval_jaxpr/gkfc,gkco->gfo/dot_general | solution.py:34
  95.5 13.6 %scatter_fusion = f32[256,8,128]{2,1,0:T(8,128)} fusion(f32[256,8,128]{2,1,0:T(8,128)} %broadcast_in_dim.17, s32[128]{0:T(128)S(1)} %compare_select_fusion.1, f32[128,8,128]{2,1,0:T(8,128)} %bitcast.38), kind=kCustom, calls=%fused_computation.3 | custom fusion | bytes 1573376 | tf_op jit(solution)/shard_map/scatter | solution.py:92
  109.1 5.6 %all-to-all-start.1 = ((f32[256,8,128]{2,1,0:T(8,128)}), f32[256,8,128]{2,1,0:T(8,128)S(1)}, u32[]{:S(2)}, u32[]{:S(2)}) async-start(f32[256,8,128]{2,1,0:T(8,128)} %scatter_fusion), calls=%async_computation.1 | async-start | bytes 2097152 | tf_op jit(solution)/shard_map/all_to_all | solution.py:96
  116.1 26.1 %all-to-all-done.1 = f32[256,8,128]{2,1,0:T(8,128)S(1)} async-done(((f32[256,8,128]{2,1,0:T(8,128)}), f32[256,8,128]{2,1,0:T(8,128)S(1)}, u32[]{:S(2)}, u32[]{:S(2)}) %all-to-all-start.1) | async-done | bytes 1048608 | tf_op jit(solution)/shard_map/all_to_all | solution.py:96
  144.9 3.0 %collective-permute-start.5 = (f32[8,1,128]{2,1,0:T(1,128)S(1)}, f32[8,1,128]{2,1,0:T(1,128)S(1)}, u32[]{:S(2)}, u32[]{:S(2)}) collective-permute-start(f32[8,1,128]{2,1,0:T(1,128)S(1)} %get-tuple-element.64), channel_id=1, source_target_pairs={{0,8},{8,16},{16,24},{1,9},{9,17},{17,25},{2,10},{10,18},{18,26},{... | collective-permute-start | bytes 12296 | tf_op jit(solution)/shard_map/ppermute | solution.py:23
  150.2 4.6 %collective-permute-start.7 = (f32[8,34,1]{2,1,0:T(8,128)S(1)}, f32[8,34,1]{2,1,0:T(8,128)S(1)}, u32[]{:S(2)}, u32[]{:S(2)}) collective-permute-start(f32[8,34,1]{2,1,0:T(8,128)S(1)} %get-tuple-element.57), channel_id=1, source_target_pairs={{0,1},{1,2},{2,3},{3,4},{4,5},{5,6},{6,7},{8,9},{9,10},{10,11},{11... | collective-permute-start | bytes 3272 | tf_op jit(solution)/shard_map/ppermute | solution.py:23
  154.7 3.0 %collective-permute-done.6 = f32[8,34,1]{2,1,0:T(8,128)S(1)} collective-permute-done((f32[8,34,1]{2,1,0:T(8,128)S(1)}, f32[8,34,1]{2,1,0:T(8,128)S(1)}, u32[]{:S(2)}, u32[]{:S(2)}) %collective-permute-start.6) | collective-permute-done | bytes 1120 | tf_op jit(solution)/shard_map/ppermute | solution.py:25
  157.7 2.7 %collective-permute-done.7 = f32[8,34,1]{2,1,0:T(8,128)S(1)} collective-permute-done((f32[8,34,1]{2,1,0:T(8,128)S(1)}, f32[8,34,1]{2,1,0:T(8,128)S(1)}, u32[]{:S(2)}, u32[]{:S(2)}) %collective-permute-start.7) | collective-permute-done | bytes 1120 | tf_op jit(solution)/shard_map/ppermute | solution.py:23
  162.0 3.0 %collective-permute-start.9 = (f32[8,1,128]{2,1,0:T(1,128)S(1)}, f32[8,1,128]{2,1,0:T(1,128)S(1)}, u32[]{:S(2)}, u32[]{:S(2)}) collective-permute-start(f32[8,1,128]{2,1,0:T(1,128)S(1)} %get-tuple-element.62), channel_id=1, source_target_pairs={{0,8},{8,16},{16,24},{1,9},{9,17},{17,25},{2,10},{10,18},{18,26},{... | collective-permute-start | bytes 12296 | tf_op jit(solution)/shard_map/ppermute | solution.py:23
  167.2 5.0 %collective-permute-start.11 = (f32[8,34,1]{2,1,0:T(8,128)S(1)}, f32[8,34,1]{2,1,0:T(8,128)S(1)}, u32[]{:S(2)}, u32[]{:S(2)}) collective-permute-start(f32[8,34,1]{2,1,0:T(8,128)S(1)} %get-tuple-element.55), channel_id=1, source_target_pairs={{0,1},{1,2},{2,3},{3,4},{4,5},{5,6},{6,7},{8,9},{9,10},{10,11},{11... | collective-permute-start | bytes 3272 | tf_op jit(solution)/shard_map/ppermute | solution.py:23
  174.9 4.4 %collective-permute-done.11 = f32[8,34,1]{2,1,0:T(8,128)S(1)} collective-permute-done((f32[8,34,1]{2,1,0:T(8,128)S(1)}, f32[8,34,1]{2,1,0:T(8,128)S(1)}, u32[]{:S(2)}, u32[]{:S(2)}) %collective-permute-start.11) | collective-permute-done | bytes 1120 | tf_op jit(solution)/shard_map/ppermute | solution.py:23
  180.8 3.0 %collective-permute-start.13 = (f32[8,1,128]{2,1,0:T(1,128)S(1)}, f32[8,1,128]{2,1,0:T(1,128)S(1)}, u32[]{:S(2)}, u32[]{:S(2)}) collective-permute-start(f32[8,1,128]{2,1,0:T(1,128)S(1)} %get-tuple-element.60), channel_id=1, source_target_pairs={{0,8},{8,16},{16,24},{1,9},{9,17},{17,25},{2,10},{10,18},{18,26},{... | collective-permute-start | bytes 12296 | tf_op jit(solution)/shard_map/ppermute | solution.py:23
  186.1 5.0 %collective-permute-start.15 = (f32[8,34,1]{2,1,0:T(8,128)S(1)}, f32[8,34,1]{2,1,0:T(8,128)S(1)}, u32[]{:S(2)}, u32[]{:S(2)}) collective-permute-start(f32[8,34,1]{2,1,0:T(8,128)S(1)} %get-tuple-element.53), channel_id=1, source_target_pairs={{0,1},{1,2},{2,3},{3,4},{4,5},{5,6},{6,7},{8,9},{9,10},{10,11},{11... | collective-permute-start | bytes 3272 | tf_op jit(solution)/shard_map/ppermute | solution.py:23
  193.7 4.5 %collective-permute-done.15 = f32[8,34,1]{2,1,0:T(8,128)S(1)} collective-permute-done((f32[8,34,1]{2,1,0:T(8,128)S(1)}, f32[8,34,1]{2,1,0:T(8,128)S(1)}, u32[]{:S(2)}, u32[]{:S(2)}) %collective-permute-start.15) | collective-permute-done | bytes 1120 | tf_op jit(solution)/shard_map/ppermute | solution.py:23
  199.6 3.0 %collective-permute-start.17 = (f32[8,1,128]{2,1,0:T(1,128)S(1)}, f32[8,1,128]{2,1,0:T(1,128)S(1)}, u32[]{:S(2)}, u32[]{:S(2)}) collective-permute-start(f32[8,1,128]{2,1,0:T(1,128)S(1)} %get-tuple-element.58), channel_id=1, source_target_pairs={{0,8},{8,16},{16,24},{1,9},{9,17},{17,25},{2,10},{10,18},{18,26},{... | collective-permute-start | bytes 12296 | tf_op jit(solution)/shard_map/ppermute | solution.py:23
  204.9 5.0 %collective-permute-start.19 = (f32[8,34,1]{2,1,0:T(8,128)S(1)}, f32[8,34,1]{2,1,0:T(8,128)S(1)}, u32[]{:S(2)}, u32[]{:S(2)}) collective-permute-start(f32[8,34,1]{2,1,0:T(8,128)S(1)} %get-tuple-element.51), channel_id=1, source_target_pairs={{0,1},{1,2},{2,3},{3,4},{4,5},{5,6},{6,7},{8,9},{9,10},{10,11},{11... | collective-permute-start | bytes 3272 | tf_op jit(solution)/shard_map/ppermute | solution.py:23
  212.5 4.5 %collective-permute-done.19 = f32[8,34,1]{2,1,0:T(8,128)S(1)} collective-permute-done((f32[8,34,1]{2,1,0:T(8,128)S(1)}, f32[8,34,1]{2,1,0:T(8,128)S(1)}, u32[]{:S(2)}, u32[]{:S(2)}) %collective-permute-start.19) | collective-permute-done | bytes 1120 | tf_op jit(solution)/shard_map/ppermute | solution.py:23
  (85 shorter events, 50.1 us)
Async XLA Ops:
  0.9 13.4 %collective-permute-start = (f32[8,1,256]{2,1,0:T(1,128)S(1)}, f32[8,1,256]{2,1,0:T(1,128)S(1)}, u32[]{:S(2)}, u32[]{:S(2)}) collective-permute-start(f32[8,1,256]{2,1,0:T(1,128)S(1)} %get-tuple-element.49), channel_id=1, source_target_pairs={{8,0},{16,8},{24,16},{0,24},{9,1},{17,9},{25,17},{1,25},{10,2},{18... | collective-permute-start | bytes 24584 | tf_op jit(solution)/shard_map/ppermute | solution.py:25
  3.3 11.0 %collective-permute-start.1 = (f32[8,1,256]{2,1,0:T(1,128)S(1)}, f32[8,1,256]{2,1,0:T(1,128)S(1)}, u32[]{:S(2)}, u32[]{:S(2)}) collective-permute-start(f32[8,1,256]{2,1,0:T(1,128)S(1)} %get-tuple-element.48), channel_id=1, source_target_pairs={{0,8},{8,16},{16,24},{24,0},{1,9},{9,17},{17,25},{25,1},{2,10},{10... | collective-permute-start | bytes 24584 | tf_op jit(solution)/shard_map/ppermute | solution.py:23
  7.5 101.6 %all-to-all-start = ((s32[32,8,1]{1,2,0:T(1,128)}), s32[32,8,1]{1,2,0:T(1,128)S(1)}, u32[]{:S(2)}, u32[]{:S(2)}) async-start(s32[32,8,1]{1,2,0:T(1,128)} %bitcast.5), calls=%async_computation | async-start | bytes 32768 | tf_op jit(solution)/shard_map/all_to_all | solution.py:97
  15.6 11.2 %collective-permute-start.2 = (f32[8,66,1]{2,1,0:T(8,128)S(1)}, f32[8,66,1]{2,1,0:T(8,128)S(1)}, u32[]{:S(2)}, u32[]{:S(2)}) collective-permute-start(f32[8,66,1]{2,1,0:T(8,128)S(1)} %get-tuple-element.43), channel_id=1, source_target_pairs={{1,0},{2,1},{3,2},{4,3},{5,4},{6,5},{7,6},{0,7},{9,8},{10,9},{11,1... | collective-permute-start | bytes 6344 | tf_op jit(solution)/shard_map/ppermute | solution.py:25
  20.2 11.5 %collective-permute-start.3 = (f32[8,66,1]{2,1,0:T(8,128)S(1)}, f32[8,66,1]{2,1,0:T(8,128)S(1)}, u32[]{:S(2)}, u32[]{:S(2)}) collective-permute-start(f32[8,66,1]{2,1,0:T(8,128)S(1)} %get-tuple-element.44), channel_id=1, source_target_pairs={{0,1},{1,2},{2,3},{3,4},{4,5},{5,6},{6,7},{7,0},{8,9},{9,10},{10,1... | collective-permute-start | bytes 6344 | tf_op jit(solution)/shard_map/ppermute | solution.py:23
  42.4 1.6 copy-start.1
  42.4 2.2 %copy-start.2 = (bf16[1,8,4,16,16,16]{5,3,1,0,4,2:T(8,128)(2,1)S(1)}, bf16[1,8,4,16,16,16]{5,3,1,0,4,2:T(8,128)(2,1)}, u32[]{:S(2)}) copy-start(bf16[1,8,4,16,16,16]{5,3,1,0,4,2:T(8,128)(2,1)} %copy.17) | copy-start | bytes 786436
  57.2 3.1 %copy-start = (bf16[16,3,256,128]{3,2,1,0:T(8,128)(2,1)S(1)}, bf16[16,3,256,128]{3,2,1,0:T(8,128)(2,1)}, u32[]{:S(2)}) copy-start(bf16[16,3,256,128]{3,2,1,0:T(8,128)(2,1)} %param.11) | copy-start | bytes 9437188
  109.1 33.0 %all-to-all-start.1 = ((f32[256,8,128]{2,1,0:T(8,128)}), f32[256,8,128]{2,1,0:T(8,128)S(1)}, u32[]{:S(2)}, u32[]{:S(2)}) async-start(f32[256,8,128]{2,1,0:T(8,128)} %scatter_fusion), calls=%async_computation.1 | async-start | bytes 2097152 | tf_op jit(solution)/shard_map/all_to_all | solution.py:96
  116.1 44.4 %copy-start.3 = (f32[32,128]{1,0:T(8,128)S(1)}, f32[32,128]{1,0:T(8,128)}, u32[]{:S(2)}) copy-start(f32[32,128]{1,0:T(8,128)} %param.10) | copy-start | bytes 49156
  143.6 4.3 %collective-permute-start.4 = (f32[8,1,128]{2,1,0:T(1,128)S(1)}, f32[8,1,128]{2,1,0:T(1,128)S(1)}, u32[]{:S(2)}, u32[]{:S(2)}) collective-permute-start(f32[8,1,128]{2,1,0:T(1,128)S(1)} %get-tuple-element.65), channel_id=1, source_target_pairs={{8,0},{16,8},{24,16},{9,1},{17,9},{25,17},{10,2},{18,10},{26,18},{... | collective-permute-start | bytes 12296 | tf_op jit(solution)/shard_map/ppermute | solution.py:25
  144.9 3.8 %collective-permute-start.5 = (f32[8,1,128]{2,1,0:T(1,128)S(1)}, f32[8,1,128]{2,1,0:T(1,128)S(1)}, u32[]{:S(2)}, u32[]{:S(2)}) collective-permute-start(f32[8,1,128]{2,1,0:T(1,128)S(1)} %get-tuple-element.64), channel_id=1, source_target_pairs={{0,8},{8,16},{16,24},{1,9},{9,17},{17,25},{2,10},{10,18},{18,26},{... | collective-permute-start | bytes 12296 | tf_op jit(solution)/shard_map/ppermute | solution.py:23
  148.9 8.8 %collective-permute-start.6 = (f32[8,34,1]{2,1,0:T(8,128)S(1)}, f32[8,34,1]{2,1,0:T(8,128)S(1)}, u32[]{:S(2)}, u32[]{:S(2)}) collective-permute-start(f32[8,34,1]{2,1,0:T(8,128)S(1)} %get-tuple-element.56), channel_id=1, source_target_pairs={{1,0},{2,1},{3,2},{4,3},{5,4},{6,5},{7,6},{9,8},{10,9},{11,10},{12... | collective-permute-start | bytes 3272 | tf_op jit(solution)/shard_map/ppermute | solution.py:25
  150.2 10.3 %collective-permute-start.7 = (f32[8,34,1]{2,1,0:T(8,128)S(1)}, f32[8,34,1]{2,1,0:T(8,128)S(1)}, u32[]{:S(2)}, u32[]{:S(2)}) collective-permute-start(f32[8,34,1]{2,1,0:T(8,128)S(1)} %get-tuple-element.57), channel_id=1, source_target_pairs={{0,1},{1,2},{2,3},{3,4},{4,5},{5,6},{6,7},{8,9},{9,10},{10,11},{11... | collective-permute-start | bytes 3272 | tf_op jit(solution)/shard_map/ppermute | solution.py:23
  160.7 4.3 %collective-permute-start.8 = (f32[8,1,128]{2,1,0:T(1,128)S(1)}, f32[8,1,128]{2,1,0:T(1,128)S(1)}, u32[]{:S(2)}, u32[]{:S(2)}) collective-permute-start(f32[8,1,128]{2,1,0:T(1,128)S(1)} %get-tuple-element.63), channel_id=1, source_target_pairs={{8,0},{16,8},{24,16},{9,1},{17,9},{25,17},{10,2},{18,10},{26,18},{... | collective-permute-start | bytes 12296 | tf_op jit(solution)/shard_map/ppermute | solution.py:25
  162.0 3.8 %collective-permute-start.9 = (f32[8,1,128]{2,1,0:T(1,128)S(1)}, f32[8,1,128]{2,1,0:T(1,128)S(1)}, u32[]{:S(2)}, u32[]{:S(2)}) collective-permute-start(f32[8,1,128]{2,1,0:T(1,128)S(1)} %get-tuple-element.62), channel_id=1, source_target_pairs={{0,8},{8,16},{16,24},{1,9},{9,17},{17,25},{2,10},{10,18},{18,26},{... | collective-permute-start | bytes 12296 | tf_op jit(solution)/shard_map/ppermute | solution.py:23
  165.9 8.9 %collective-permute-start.10 = (f32[8,34,1]{2,1,0:T(8,128)S(1)}, f32[8,34,1]{2,1,0:T(8,128)S(1)}, u32[]{:S(2)}, u32[]{:S(2)}) collective-permute-start(f32[8,34,1]{2,1,0:T(8,128)S(1)} %get-tuple-element.54), channel_id=1, source_target_pairs={{1,0},{2,1},{3,2},{4,3},{5,4},{6,5},{7,6},{9,8},{10,9},{11,10},{12... | collective-permute-start | bytes 3272 | tf_op jit(solution)/shard_map/ppermute | solution.py:25
  167.2 12.0 %collective-permute-start.11 = (f32[8,34,1]{2,1,0:T(8,128)S(1)}, f32[8,34,1]{2,1,0:T(8,128)S(1)}, u32[]{:S(2)}, u32[]{:S(2)}) collective-permute-start(f32[8,34,1]{2,1,0:T(8,128)S(1)} %get-tuple-element.55), channel_id=1, source_target_pairs={{0,1},{1,2},{2,3},{3,4},{4,5},{5,6},{6,7},{8,9},{9,10},{10,11},{11... | collective-permute-start | bytes 3272 | tf_op jit(solution)/shard_map/ppermute | solution.py:23
  179.5 4.3 %collective-permute-start.12 = (f32[8,1,128]{2,1,0:T(1,128)S(1)}, f32[8,1,128]{2,1,0:T(1,128)S(1)}, u32[]{:S(2)}, u32[]{:S(2)}) collective-permute-start(f32[8,1,128]{2,1,0:T(1,128)S(1)} %get-tuple-element.61), channel_id=1, source_target_pairs={{8,0},{16,8},{24,16},{9,1},{17,9},{25,17},{10,2},{18,10},{26,18},{... | collective-permute-start | bytes 12296 | tf_op jit(solution)/shard_map/ppermute | solution.py:25
  180.8 3.8 %collective-permute-start.13 = (f32[8,1,128]{2,1,0:T(1,128)S(1)}, f32[8,1,128]{2,1,0:T(1,128)S(1)}, u32[]{:S(2)}, u32[]{:S(2)}) collective-permute-start(f32[8,1,128]{2,1,0:T(1,128)S(1)} %get-tuple-element.60), channel_id=1, source_target_pairs={{0,8},{8,16},{16,24},{1,9},{9,17},{17,25},{2,10},{10,18},{18,26},{... | collective-permute-start | bytes 12296 | tf_op jit(solution)/shard_map/ppermute | solution.py:23
  184.8 8.9 %collective-permute-start.14 = (f32[8,34,1]{2,1,0:T(8,128)S(1)}, f32[8,34,1]{2,1,0:T(8,128)S(1)}, u32[]{:S(2)}, u32[]{:S(2)}) collective-permute-start(f32[8,34,1]{2,1,0:T(8,128)S(1)} %get-tuple-element.52), channel_id=1, source_target_pairs={{1,0},{2,1},{3,2},{4,3},{5,4},{6,5},{7,6},{9,8},{10,9},{11,10},{12... | collective-permute-start | bytes 3272 | tf_op jit(solution)/shard_map/ppermute | solution.py:25
  186.1 12.1 %collective-permute-start.15 = (f32[8,34,1]{2,1,0:T(8,128)S(1)}, f32[8,34,1]{2,1,0:T(8,128)S(1)}, u32[]{:S(2)}, u32[]{:S(2)}) collective-permute-start(f32[8,34,1]{2,1,0:T(8,128)S(1)} %get-tuple-element.53), channel_id=1, source_target_pairs={{0,1},{1,2},{2,3},{3,4},{4,5},{5,6},{6,7},{8,9},{9,10},{10,11},{11... | collective-permute-start | bytes 3272 | tf_op jit(solution)/shard_map/ppermute | solution.py:23
  198.3 4.3 %collective-permute-start.16 = (f32[8,1,128]{2,1,0:T(1,128)S(1)}, f32[8,1,128]{2,1,0:T(1,128)S(1)}, u32[]{:S(2)}, u32[]{:S(2)}) collective-permute-start(f32[8,1,128]{2,1,0:T(1,128)S(1)} %get-tuple-element.59), channel_id=1, source_target_pairs={{8,0},{16,8},{24,16},{9,1},{17,9},{25,17},{10,2},{18,10},{26,18},{... | collective-permute-start | bytes 12296 | tf_op jit(solution)/shard_map/ppermute | solution.py:25
  199.6 3.8 %collective-permute-start.17 = (f32[8,1,128]{2,1,0:T(1,128)S(1)}, f32[8,1,128]{2,1,0:T(1,128)S(1)}, u32[]{:S(2)}, u32[]{:S(2)}) collective-permute-start(f32[8,1,128]{2,1,0:T(1,128)S(1)} %get-tuple-element.58), channel_id=1, source_target_pairs={{0,8},{8,16},{16,24},{1,9},{9,17},{17,25},{2,10},{10,18},{18,26},{... | collective-permute-start | bytes 12296 | tf_op jit(solution)/shard_map/ppermute | solution.py:23
  203.6 8.9 %collective-permute-start.18 = (f32[8,34,1]{2,1,0:T(8,128)S(1)}, f32[8,34,1]{2,1,0:T(8,128)S(1)}, u32[]{:S(2)}, u32[]{:S(2)}) collective-permute-start(f32[8,34,1]{2,1,0:T(8,128)S(1)} %get-tuple-element.50), channel_id=1, source_target_pairs={{1,0},{2,1},{3,2},{4,3},{5,4},{6,5},{7,6},{9,8},{10,9},{11,10},{12... | collective-permute-start | bytes 3272 | tf_op jit(solution)/shard_map/ppermute | solution.py:25
  204.9 12.1 %collective-permute-start.19 = (f32[8,34,1]{2,1,0:T(8,128)S(1)}, f32[8,34,1]{2,1,0:T(8,128)S(1)}, u32[]{:S(2)}, u32[]{:S(2)}) collective-permute-start(f32[8,34,1]{2,1,0:T(8,128)S(1)} %get-tuple-element.51), channel_id=1, source_target_pairs={{0,1},{1,2},{2,3},{3,4},{4,5},{5,6},{6,7},{8,9},{9,10},{10,11},{11... | collective-permute-start | bytes 3272 | tf_op jit(solution)/shard_map/ppermute | solution.py:23
where the time goes:
time: 219 us; the launch traced here: 218 us
  waiting for transfers between devices  66.8 us (31%)
  starting transfers between devices  60.8 us (28%)
  local copies, waits for them, and re-layouts  58 us (26%)
  matrix products  18.6 us (8%)
  other arithmetic  13.1 us (6%)
    ppermute x10, starting transfers between devices, extended(): lax.ppermute(tail, axis, [(i, (i + 1) % count) for i in range(ends)])  31.7 us
    all_to_all x1, waiting for transfers between devices, local(): lax.all_to_all(outgoing, ('gx', 'gy'), split_axis=0, concat_axis=0, tiled...  26.1 us
    ppermute x10, waiting for transfers between devices, extended(): lax.ppermute(tail, axis, [(i, (i + 1) % count) for i in range(ends)])  24.1 us
    dot_general x4, matrix products, block_products(): jnp.einsum('gkfc,gkco->gfo', source_part, bank_part, preferred_element_ty...  18 us
    ppermute x10, starting transfers between devices, extended(): lax.ppermute(head, axis, [((i + 1) % count, i) for i in range(ends)])  17.4 us
    ppermute x10, waiting for transfers between devices, extended(): lax.ppermute(head, axis, [((i + 1) % count, i) for i in range(ends)])  16.6 us
    gather x4, local copies, waits for them, and re-layouts, block_products(): bank_part = remap_bank[jnp.maximum(weight_ids, 0)]  16 us
    scatter x1, local copies, waits for them, and re-layouts, local(): outgoing = jnp.zeros((slot_count,) + partial_value.shape[1:], jnp.float32...  13.6 us
  transfers between devices with their start and end apart: 22, of which 15 were waited for; matrix products, arithmetic and copies ran while one was open for 38% of the time, Pallas kernels for 0%

commit v1 on v0

v1 whole, which is shorter than its diff:
```python
import functools

import jax
import jax.numpy as jnp
from jax import lax
from jax.experimental import pallas as pl
from jax.experimental.pallas import tpu as pltpu
from jax.sharding import PartitionSpec as P

TILE_X = 16
TILE_Y = 16
OTILE_X = 8
OTILE_Y = 16
SWEEPS = 4
LANES = 128
MESH = pl.DeviceIdType.MESH


def lane_of(shape):
    return lax.broadcasted_iota(jnp.int32, shape, len(shape) - 1)


def block_transpose(parts, width):
    parts = list(parts)
    block = lane_of(parts[0].shape) // width
    step = 1
    while step < len(parts):
        keep = (block & step) == 0
        for i in range(len(parts)):
            if i & step == 0:
                j = i | step
                low, high = parts[i], parts[j]
                parts[i] = jnp.where(keep, low, pltpu.roll(high, step * width, 1))
                parts[j] = jnp.where(keep, pltpu.roll(low, LANES - step * width, 1), high)
        step *= 2
    return parts


def kernel(
    nx, ny, cap,
    flux, diff, bank, own, src, tgt, wgt,
    out,
    bank_v, xs, xmat, prod, table_v, table_s, meta_s, meta_r, sent, got,
    row_s, row_r, col_s, col_r, d_edge, d_corner, d_row, u, pack_s, u_edge, u_corner, u_row,
    bank_sem, table_sem, a_send, a_recv, m_send, m_recv, h_send, h_recv,
):
    n = nx * ny
    fields, rows, cols = flux.shape
    nwb = bank.shape[0]
    tiles_x, tiles_y = rows // TILE_X, cols // TILE_Y
    tiles = tiles_x * tiles_y
    orows = diff.shape[0]
    oty = diff.shape[1] // OTILE_Y
    otx = orows // OTILE_X
    span = cap * fields
    gx, gy = lax.axis_index("gx"), lax.axis_index("gy")
    me = gx * ny + gy
    up, down = lax.rem(gx + nx - 1, nx), lax.rem(gx + 1, nx)
    left, right = lax.rem(gy + ny - 1, ny), lax.rem(gy + 1, ny)

    barrier = pltpu.get_barrier_semaphore()

    def greet(k, c):
        d = lax.rem(me + k, n)
        pl.semaphore_signal(barrier, inc=1, device_id=(d // ny, lax.rem(d, ny)), device_id_type=MESH)
        return c

    lax.fori_loop(1, n, greet, 0)
    bank_copy = pltpu.make_async_copy(bank, bank_v, bank_sem)
    bank_copy.start()

    records = own.shape[1]
    owner_i = lax.broadcasted_iota(jnp.int32, (n, records), 0)
    member = own[...] == owner_i
    lower = lax.broadcasted_iota(jnp.int32, (records, records), 0) < lane_of((records, records))
    before = jnp.dot(
        member.astype(jnp.bfloat16), lower.astype(jnp.bfloat16), preferred_element_type=jnp.float32
    )
    source, target = src[...], tgt[...]
    code = (wgt[...] * tiles + lax.rem(source, tiles_y) * tiles_x + source // tiles_y).astype(jnp.float32)
    aim = (lax.rem(target, oty) * (fields * otx) + target // oty).astype(jnp.float32)
    lane = lane_of((n, LANES))
    slot_lane = lax.rem(lane, span) // fields
    field_lane = (lax.rem(lane, fields) * otx).astype(jnp.float32)
    table = jnp.zeros((n, LANES), jnp.float32)
    meta = jnp.full((n, LANES), -1.0, jnp.float32)
    for k in range(cap):
        hit = jnp.logical_and(member, before == k)
        code_k = jnp.sum(jnp.where(hit, code, 0.0), axis=1, keepdims=True)
        aim_k = jnp.sum(jnp.where(hit, aim + 1.0, 0.0), axis=1, keepdims=True) - 1.0
        table = jnp.where(lane == k, code_k, table)
        filled = jnp.where(aim_k >= 0.0, aim_k + field_lane, -1.0)
        meta = jnp.where(slot_lane == k, filled, meta)
    table_v[...] = table.astype(jnp.int32)
    table_copy = pltpu.make_async_copy(table_v, table_s, table_sem)
    table_copy.start()
    for o in range(n):
        meta_s[o] = meta[o : o + 1, :]
    meta_r[me] = meta_s[me]

    for f in range(fields):
        for h in range(2):
            xs[0, h, f * rows : (f + 1) * rows, :] = flux[f, :, h * LANES : (h + 1) * LANES]
    lane_c = lane_of((rows, LANES))
    first = jnp.zeros((rows, LANES), jnp.float32)
    last = jnp.zeros((rows, LANES), jnp.float32)
    for f in range(fields):
        a = flux[f, :, 0:LANES]
        b = flux[f, :, cols - LANES : cols]
        first = jnp.where(lane_c == f, pltpu.roll(a, f, 1) if f else a, first)
        last = jnp.where(lane_c == f, pltpu.roll(b, f + 1, 1), last)
    col_s[0] = first
    col_s[1] = last
    for h in range(2):
        row_s[0, h] = xs[0, h, pl.ds(0, fields, stride=rows), :]
        row_s[1, h] = xs[0, h, pl.ds(rows - 1, fields, stride=rows), :]

    pl.semaphore_wait(barrier, n - 1)

    def remote(a, b, k, x, y):
        return pltpu.make_async_remote_copy(
            src_ref=a, dst_ref=b, send_sem=h_send.at[k], recv_sem=h_recv.at[k],
            device_id=(x, y), device_id_type=MESH,
        )

    flux_copies = [
        remote(row_s.at[0], row_r.at[1], 0, up, gy),
        remote(row_s.at[1], row_r.at[0], 1, down, gy),
        remote(col_s.at[0], col_r.at[1], 2, gx, left),
        remote(col_s.at[1], col_r.at[0], 3, gx, right),
    ]
    for c in flux_copies:
        c.start()

    def halo_copies(base, edge0, edge1, row0, row1, edge, corner, row):
        low = pl.ds(0, 8)
        high = pl.ds(orows - 8, 8)
        return [
            remote(edge0, edge.at[1], base, gx, left),
            remote(edge1, edge.at[0], base + 1, gx, right),
            remote(row0, row.at[1], base + 2, up, gy),
            remote(row1, row.at[0], base + 3, down, gy),
            remote(edge0.at[low], corner.at[1, 1], base + 4, up, left),
            remote(edge0.at[high], corner.at[0, 1], base + 5, down, left),
            remote(edge1.at[low], corner.at[1, 0], base + 6, up, right),
            remote(edge1.at[high], corner.at[0, 0], base + 7, down, right),
        ]

    diff_copies = halo_copies(
        4, diff, diff, diff.at[pl.ds(0, 8)], diff.at[pl.ds(orows - 8, 8)], d_edge, d_corner, d_row
    )
    for c in diff_copies:
        c.start()

    def meta_to(d):
        return pltpu.make_async_remote_copy(
            src_ref=meta_s.at[d], dst_ref=meta_r.at[me], send_sem=m_send.at[d], recv_sem=m_recv.at[me],
            device_id=(d // ny, lax.rem(d, ny)), device_id_type=MESH,
        )

    def data_to(d):
        return pltpu.make_async_remote_copy(
            src_ref=sent.at[d], dst_ref=got.at[me], send_sem=a_send.at[d], recv_sem=a_recv.at[me],
            device_id=(d // ny, lax.rem(d, ny)), device_id_type=MESH,
        )

    def send_meta(k, c):
        meta_to(lax.rem(me + k, n)).start()
        return c

    lax.fori_loop(1, n, send_meta, 0)

    for c in flux_copies:
        c.wait()
    row_i = lax.broadcasted_iota(jnp.int32, (rows, LANES), 0)
    for f in range(fields):
        halves = [flux[f, :, h * LANES : (h + 1) * LANES] for h in range(2)]
        ends = (
            pltpu.roll(col_r[0], LANES - f, 1) if f else col_r[0],
            pltpu.roll(col_r[1], LANES - 1 - f, 1),
        )
        to_right = [pltpu.roll(x, 1, 1) for x in halves]
        to_left = [pltpu.roll(x, LANES - 1, 1) for x in halves]
        at_first, at_last = lane_c == 0, lane_c == LANES - 1
        before_y = [jnp.where(at_first, ends[0], to_right[0]), jnp.where(at_first, to_right[0], to_right[1])]
        after_y = [jnp.where(at_last, to_left[1], to_left[0]), jnp.where(at_last, ends[1], to_left[1])]
        for h in range(2):
            x = halves[h]
            above = jnp.where(row_i == 0, row_r[0, h, f : f + 1, :], pltpu.roll(x, 1, 0))
            below = jnp.where(row_i == rows - 1, row_r[1, h, f : f + 1, :], pltpu.roll(x, rows - 1, 0))
            xs[1, h, f * rows : (f + 1) * rows, :] = (below - above) * 0.5
            xs[2, h, f * rows : (f + 1) * rows, :] = (after_y[h] - before_y[h]) * 0.5

    per = LANES // TILE_Y
    halfx = TILE_X // per
    tile_rows = tiles_x * fields
    for c in range(3):
        for h in range(2):
            for g in range(halfx):
                parts = [
                    jnp.concatenate(
                        [
                            xs[c, h, pl.ds(t * TILE_X + g * per + a, fields, stride=rows), :]
                            for t in range(tiles_x)
                        ],
                        axis=0,
                    )
                    for a in range(per)
                ]
                parts = block_transpose(parts, TILE_Y)
                at = (c * halfx + g) * LANES
                for t in range(per):
                    j = h * per + t
                    xmat[j * tile_rows : (j + 1) * tile_rows, at : at + LANES] = parts[t].astype(jnp.bfloat16)

    bank_copy.wait()

    def products(p, c):
        pair = jnp.concatenate([bank_v[2 * p], bank_v[2 * p + 1]], axis=1)
        got_pair = jnp.dot(xmat[...], pair, preferred_element_type=jnp.float32)
        prod[pl.ds(2 * p * tiles, tiles)] = got_pair[:, :LANES].reshape(tiles, fields, LANES)
        prod[pl.ds((2 * p + 1) * tiles, tiles)] = got_pair[:, LANES:].reshape(tiles, fields, LANES)
        return c

    lax.fori_loop(0, nwb // 2, products, 0)
    table_copy.wait()

    def record(d, s):
        return prod[jnp.clip(table_s[d, s], 0, nwb * tiles - 1)]

    def fill(d, ref):
        for s in range(0, cap, 2):
            pair = jnp.concatenate([record(d, s), record(d, s + 1)], axis=0)
            ref[d, s * fields : (s + 2) * fields, :] = pair.astype(jnp.bfloat16)

    def send_data(k, c):
        d = lax.rem(me + k, n)
        fill(d, sent)
        data_to(d).start()
        return c

    lax.fori_loop(1, n, send_data, 0)
    fill(me, got)

    group = max(1, 2 * LANES // span)
    cells = fields * otx * oty
    shares = LANES // span
    cell_i = lax.broadcasted_iota(jnp.int32, (cells, LANES), 0).astype(jnp.float32)
    part_lane = lane_of((1, LANES)) // span

    def collect(q, total):
        def arrive(i, c):
            s = q * group + i

            @pl.when(s != me)
            def _():
                pltpu.make_async_remote_copy(
                    src_ref=meta_s.at[s], dst_ref=meta_r.at[s], send_sem=m_send.at[s], recv_sem=m_recv.at[s],
                    device_id=(s // ny, lax.rem(s, ny)), device_id_type=MESH,
                ).wait_recv()
                pltpu.make_async_remote_copy(
                    src_ref=sent.at[s], dst_ref=got.at[s], send_sem=a_send.at[s], recv_sem=a_recv.at[s],
                    device_id=(s // ny, lax.rem(s, ny)), device_id_type=MESH,
                ).wait_recv()

            return c

        lax.fori_loop(0, group, arrive, 0)
        hots = []
        for b in range(group // shares):
            aims = meta_r[q * group + b * shares]
            for i in range(1, shares):
                aims = jnp.where(part_lane == i, meta_r[q * group + b * shares + i], aims)
            hots.append(jnp.where(cell_i == aims, 1.0, 0.0).astype(jnp.bfloat16))
        hot = jnp.concatenate(hots, axis=1)
        data = got[pl.ds(q * group, group)].reshape(group * span, LANES)
        return total + jnp.dot(hot, data, preferred_element_type=jnp.float32)

    total = lax.fori_loop(0, n // group, collect, jnp.zeros((cells, LANES), jnp.float32))
    high = fields * otx
    parts = block_transpose([total[t * high : (t + 1) * high, :] for t in range(oty)], OTILE_Y)
    for a in range(OTILE_X):
        u[pl.ds(a, high, stride=OTILE_X), :] = parts[a]

    lane_o = lane_of((orows, LANES))
    packed = [jnp.zeros((orows, LANES), jnp.float32) for _ in range(2)]
    for f in range(fields):
        block = u[f * orows : (f + 1) * orows, :]
        shift = f * SWEEPS
        rolled = (pltpu.roll(block, shift, 1), pltpu.roll(block, LANES - shift, 1)) if f else (block, block)
        mine = (lane_o // SWEEPS == f, (LANES - 1 - lane_o) // SWEEPS == f)
        packed = [jnp.where(mine[e], rolled[e], packed[e]) for e in range(2)]
        pack_s[2, f * 8 : f * 8 + 8, :] = block[0:8]
        pack_s[3, f * 8 : f * 8 + 8, :] = block[orows - 8 : orows]
    pack_s[0, 0:orows, :] = packed[0]
    pack_s[1, 0:orows, :] = packed[1]
    ocean_copies = halo_copies(
        12,
        pack_s.at[0, pl.ds(0, orows)],
        pack_s.at[1, pl.ds(0, orows)],
        pack_s.at[2, pl.ds(0, fields * 8)],
        pack_s.at[3, pl.ds(0, fields * 8)],
        u_edge, u_corner, u_row,
    )
    for c in ocean_copies:
        c.start()

    for c in diff_copies:
        c.wait()

    has = (gx > 0, gx < nx - 1, gy > 0, gy < ny - 1)
    tail_lane = lane_of((8, LANES)) < LANES // 2
    tail_row = lax.broadcasted_iota(jnp.int32, (8, LANES), 0) < 4
    wide_lane = lane_o < LANES // 2
    row_ok = jnp.where(tail_row, has[1].astype(jnp.float32), has[0].astype(jnp.float32))
    col_ok = jnp.where(wide_lane, has[3].astype(jnp.float32), has[2].astype(jnp.float32))
    both_ok = row_ok * col_ok[0:8]
    d_tail = jnp.where(tail_row, d_row[1], d_row[0]) * row_ok
    d_side = jnp.where(wide_lane, d_edge[1], d_edge[0]) * col_ok
    d_both = (
        jnp.where(
            tail_lane,
            jnp.where(tail_row, d_corner[1, 1], d_corner[0, 1]),
            jnp.where(tail_row, d_corner[1, 0], d_corner[0, 0]),
        )
        * both_ok
    )
    d = [
        jnp.concatenate([diff[...], d_tail], axis=0),
        jnp.concatenate([d_side, d_both], axis=0),
    ]
    for c in ocean_copies:
        c.wait()
    side = [
        jnp.concatenate([u_edge[e], jnp.where(tail_row, u_corner[1, e], u_corner[0, e])], axis=0)
        for e in range(2)
    ]
    ext = orows + 8
    lane_e = lane_of((ext, LANES))
    side_ok = jnp.concatenate([col_ok, both_ok], axis=0)
    at_first, at_last = lane_e == 0, lane_e == LANES - 1
    for f in range(fields):
        shift = f * SWEEPS
        tail = jnp.where(tail_row, u_row[1, f * 8 : f * 8 + 8, :], u_row[0, f * 8 : f * 8 + 8, :]) * row_ok
        rolled = (
            (pltpu.roll(side[1], LANES - shift, 1), pltpu.roll(side[0], shift, 1)) if f else (side[1], side[0])
        )
        x = [
            jnp.concatenate([u[f * orows : (f + 1) * orows, :], tail], axis=0),
            jnp.where(lane_e < LANES // 2, rolled[0], rolled[1]) * side_ok,
        ]
        for sweep in range(SWEEPS):
            to_right = [pltpu.roll(v, 1, 1) for v in x]
            to_left = [pltpu.roll(v, LANES - 1, 1) for v in x]
            beside = [
                jnp.where(at_first, to_right[1 - h], to_right[h])
                + jnp.where(at_last, to_left[1 - h], to_left[h])
                + pltpu.roll(x[h], 1, 0)
                + pltpu.roll(x[h], ext - 1, 0)
                for h in range(2)
            ]
            x = [x[h] + d[h] * (beside[h] - 4.0 * x[h]) for h in range(2)]
        out[f] = x[0][0:orows, :]

    def settle(k, c):
        t = lax.rem(me + k, n)
        meta_to(t).wait_send()
        data_to(t).wait_send()
        return c

    lax.fori_loop(1, n, settle, 0)


def local(nx, ny, flux, diffusivity, remap_bank, rec_owner, rec_source, rec_target, rec_weight):
    n = nx * ny
    fields, rows, cols = flux.shape
    orows, ocols = diffusivity.shape
    records = rec_owner.shape[0]
    cap = max(2, 2 * records // n)
    nwb = remap_bank.shape[0]
    depth = 3 * TILE_X * TILE_Y
    tiles = rows // TILE_X * (cols // TILE_Y)
    span = cap * fields
    f32, bf16 = jnp.float32, jnp.bfloat16
    v = pltpu.VMEM
    dma = pltpu.SemaphoreType.DMA
    vm = pl.BlockSpec(memory_space=pltpu.VMEM)
    flat = [x.reshape(1, records) for x in (rec_owner, rec_source, rec_target, rec_weight)]
    return pl.pallas_call(
        functools.partial(kernel, nx, ny, cap),
        out_shape=jax.ShapeDtypeStruct((fields, orows, ocols), f32),
        in_specs=[vm, vm, pl.BlockSpec(memory_space=pl.ANY)] + [vm] * 4,
        out_specs=vm,
        scratch_shapes=[
            v((nwb, depth, LANES), bf16),
            v((3, 2, (fields + 1) * rows, LANES), f32),
            v((tiles * fields, depth), bf16),
            v((nwb * tiles, fields, LANES), f32),
            v((n, LANES), jnp.int32),
            pltpu.SMEM((n, LANES), jnp.int32),
            v((n, 1, LANES), f32),
            v((n, 1, LANES), f32),
            v((n, span, LANES), bf16),
            v((n, span, LANES), bf16),
            v((2, 2, fields, LANES), f32),
            v((2, 2, fields, LANES), f32),
            v((2, rows, LANES), f32),
            v((2, rows, LANES), f32),
            v((2, orows, LANES), f32),
            v((2, 2, 8, LANES), f32),
            v((2, 8, LANES), f32),
            v((fields * orows + OTILE_X, LANES), f32),
            v((4, max(orows, fields * 8), LANES), f32),
            v((2, orows, LANES), f32),
            v((2, 2, 8, LANES), f32),
            v((2, fields * 8, LANES), f32),
            dma, dma,
            dma((n,)), dma((n,)), dma((n,)), dma((n,)),
            dma((20,)), dma((20,)),
        ],
        compiler_params=pltpu.CompilerParams(
            collective_id=0, has_side_effects=True, vmem_limit_bytes=40 * 1024 * 1024
        ),
    )(flux, diffusivity, remap_bank.reshape(nwb, depth, LANES), *flat)


def solution(mesh):
    in_specs = (
        P(None, "gx", "gy"),
        P("gx", "gy"),
        P(),
        P(("gx", "gy")),
        P(("gx", "gy")),
        P(("gx", "gy")),
        P(("gx", "gy")),
    )
    out_specs = P(None, "gx", "gy")
    body = functools.partial(local, mesh.shape["gx"], mesh.shape["gy"])
    return jax.shard_map(body, mesh=mesh, in_specs=in_specs, out_specs=out_specs, check_vma=False)
```

time: 219 us -> 47.3 us (0.22)
  waiting for transfers between devices: 66.8 us -> 0 us
  starting transfers between devices: 60.8 us -> 0 us
  local copies, waits for them, and re-layouts: 58 us -> 6.92 us
  Pallas kernels: 0 us -> 40.1 us
  matrix products: 18.6 us -> 0 us
  other arithmetic: 13.1 us -> 0 us
    ppermute x20 -> x0, starting transfers between devices: 49.1 us -> none  [the longest x10 31.7 us: extended(): lax.ppermute(tail, axis, [(i, (i + 1) % count) for i in range(ends)])]
    ppermute x20 -> x0, waiting for transfers between devices: 40.7 us -> none  [the longest x10 24.1 us: extended(): lax.ppermute(tail, axis, [(i, (i + 1) % count) for i in range(ends)])]
    pallas_call x0 -> x1, Pallas kernels: none -> 40.1 us  [local(): pl.pallas_call(functools.partial(kernel, nx, ny, cap), out_shape=jax.Shap...]
    all_to_all x2 -> x0, waiting for transfers between devices: 26.1 us -> none  [the longest x1 26.1 us: local(): lax.all_to_all(outgoing, ('gx', 'gy'), split_axis=0, concat_axis=0, tiled...]
    gather x5 -> x0, local copies, waits for them, and re-layouts: 19.1 us -> none  [the longest x4 16 us: block_products(): bank_part = remap_bank[jnp.maximum(weight_ids, 0)]]
    dot_general x5 -> x0, matrix products: 18.6 us -> none  [the longest x4 18 us: block_products(): jnp.einsum('gkfc,gkco->gfo', source_part, bank_part, preferred_element_ty...]
    scatter x2 -> x0, local copies, waits for them, and re-layouts: 14.7 us -> none  [the longest x1 13.6 us: local(): outgoing = jnp.zeros((slot_count,) + partial_value.shape[1:], jnp.float32...]
    all_to_all x2 -> x0, starting transfers between devices: 11.7 us -> none  [the longest x1 6.1 us: local(): lax.all_to_all(aimed_tile, ('gx', 'gy'), split_axis=0, concat_axis=0, til...]
  transfers between devices with their start and end apart: 22 -> 0, of which waited for: 15 -> 0; matrix products, arithmetic and copies ran while one was open for 38% -> 0% of each run, Pallas kernels for 0% -> 0%
where the time goes in v1:
time: 47.3 us; the launch traced here: 47 us
  Pallas kernels  40.1 us (85%)
  local copies, waits for them, and re-layouts  6.92 us (15%)
    pallas_call x1, Pallas kernels, local(): pl.pallas_call(functools.partial(kernel, nx, ny, cap), out_shape=jax.Shap...  40.1 us
    unnamed x15, local copies, waits for them, and re-layouts  6.92 us

profile of v1, /device:TPU:0, one launch (start us, length us, event | category | flops | bytes accessed | tf_op | source)
XLA Modules:
  0.0 47.0 jit_solution(2661620123642046860)
XLA Ops:
  0.0 0.0 copy-start
  0.0 1.9 %copy-done = bf16[16,3,256,128]{3,2,1,0:T(8,128)(2,1)S(1)} copy-done((bf16[16,3,256,128]{3,2,1,0:T(8,128)(2,1)S(1)}, bf16[16,3,256,128]{3,2,1,0:T(8,128)(2,1)}, u32[]{:S(2)}) %copy-start) | copy-done | bytes 3145752
  1.9 0.0 copy-start.1
  1.9 1.0 %copy-done.1 = f32[8,64,256]{2,1,0:T(8,128)S(1)} copy-done((f32[8,64,256]{2,1,0:T(8,128)S(1)}, f32[8,64,256]{2,1,0:T(8,128)}, u32[]{:S(2)}) %copy-start.1) | copy-done | bytes 524312
  2.9 0.0 copy-start.2
  2.9 0.7 %copy-done.2 = f32[32,128]{1,0:T(8,128)S(1)} copy-done((f32[32,128]{1,0:T(8,128)S(1)}, f32[32,128]{1,0:T(8,128)}, u32[]{:S(2)}) %copy-start.2) | copy-done | bytes 16408
  3.7 0.0 copy-start.3
  3.7 0.7 %copy-done.3 = s32[128]{0:T(128)S(1)} copy-done((s32[128]{0:T(128)S(1)}, s32[128]{0:T(128)}, u32[]{:S(2)}) %copy-start.3) | copy-done | bytes 536
  4.3 0.0 copy-start.4
  4.3 0.7 %copy-done.4 = s32[128]{0:T(128)S(1)} copy-done((s32[128]{0:T(128)S(1)}, s32[128]{0:T(128)}, u32[]{:S(2)}) %copy-start.4) | copy-done | bytes 536
  5.0 0.0 copy-start.5
  5.0 0.7 %copy-done.5 = s32[128]{0:T(128)S(1)} copy-done((s32[128]{0:T(128)S(1)}, s32[128]{0:T(128)}, u32[]{:S(2)}) %copy-start.5) | copy-done | bytes 536
  5.6 0.0 copy-start.6
  5.6 0.7 %copy-done.6 = s32[128]{0:T(128)S(1)} copy-done((s32[128]{0:T(128)S(1)}, s32[128]{0:T(128)}, u32[]{:S(2)}) %copy-start.6) | copy-done | bytes 536
  6.3 40.1 %shard_map.73 = f32[8,32,128]{2,1,0:T(8,128)S(1)} custom-call(f32[8,64,256]{2,1,0:T(8,128)S(1)} %copy-done.1, f32[32,128]{1,0:T(8,128)S(1)} %copy-done.2, bf16[16,768,128]{2,1,0:T(8,128)(2,1)S(1)} %bitcast.5, s32[1,128]{1,0:T(1,128)S(1)} %bitcast.6, s32[1,128]{1,0:T(1,128)S(1)} %bitcast.7, s32[1,128]{1,0:T(1,128)S(1)} %bitcast.8, s32[1,128]{1,0:T(1,128)S(1)} %bitcast.9), custom_call_target="tpu_custom_call" | custom-call | tf_op jit(solution)/shard_map/pallas_call | solution.py:389
  46.4 0.7 %copy.9 = f32[8,32,128]{2,1,0:T(8,128)} copy(f32[8,32,128]{2,1,0:T(8,128)S(1)} %shard_map.73) | data formatting | bytes 262144
Async XLA Ops:
  0.0 1.9 %copy-start = (bf16[16,3,256,128]{3,2,1,0:T(8,128)(2,1)S(1)}, bf16[16,3,256,128]{3,2,1,0:T(8,128)(2,1)}, u32[]{:S(2)}) copy-start(bf16[16,3,256,128]{3,2,1,0:T(8,128)(2,1)} %param.9) | copy-start | bytes 9437188
  1.9 1.0 %copy-start.1 = (f32[8,64,256]{2,1,0:T(8,128)S(1)}, f32[8,64,256]{2,1,0:T(8,128)}, u32[]{:S(2)}) copy-start(f32[8,64,256]{2,1,0:T(8,128)} %flux.1) | copy-start | bytes 1572868
  2.9 0.7 %copy-start.2 = (f32[32,128]{1,0:T(8,128)S(1)}, f32[32,128]{1,0:T(8,128)}, u32[]{:S(2)}) copy-start(f32[32,128]{1,0:T(8,128)} %diff.1) | copy-start | bytes 49156
  3.7 0.7 %copy-start.3 = (s32[128]{0:T(128)S(1)}, s32[128]{0:T(128)}, u32[]{:S(2)}) copy-start(s32[128]{0:T(128)} %param.10) | copy-start | bytes 1540
  4.3 0.7 %copy-start.4 = (s32[128]{0:T(128)S(1)}, s32[128]{0:T(128)}, u32[]{:S(2)}) copy-start(s32[128]{0:T(128)} %param.11) | copy-start | bytes 1540
  5.0 0.7 %copy-start.5 = (s32[128]{0:T(128)S(1)}, s32[128]{0:T(128)}, u32[]{:S(2)}) copy-start(s32[128]{0:T(128)} %param.12) | copy-start | bytes 1540
  5.6 0.7 %copy-start.6 = (s32[128]{0:T(128)S(1)}, s32[128]{0:T(128)}, u32[]{:S(2)}) copy-start(s32[128]{0:T(128)} %param.13) | copy-start | bytes 1540

commit v2 on v1

--- a/solution.py
+++ b/solution.py
@@ -38,8 +38,9 @@
 
 def kernel(
     nx, ny, cap,
-    flux, diff, bank, own, src, tgt, wgt,
+    flux_h, diff_h, bank, own_h, src_h, tgt_h, wgt_h,
     out,
+    flux, diff, recs, in_sem,
     bank_v, xs, xmat, prod, table_v, table_s, meta_s, meta_r, sent, got,
     row_s, row_r, col_s, col_r, d_edge, d_corner, d_row, u, pack_s, u_edge, u_corner, u_row,
     bank_sem, table_sem, a_send, a_recv, m_send, m_recv, h_send, h_recv,
@@ -60,24 +61,102 @@
 
     barrier = pltpu.get_barrier_semaphore()
 
-    def greet(k, c):
-        d = lax.rem(me + k, n)
-        pl.semaphore_signal(barrier, inc=1, device_id=(d // ny, lax.rem(d, ny)), device_id_type=MESH)
-        return c
-
-    lax.fori_loop(1, n, greet, 0)
+    y_order = [o for k in range(ny // 2 + 1) for o in sorted({ny // 2 - k, ny // 2 + k}) if o < ny]
+    y_at = [gy if o == 0 else lax.rem(gy + o, ny) for o in y_order]
+
+    def each_other(act):
+        def one_row(i, c):
+            x = lax.rem(gx + i, nx)
+            for o, y in zip(y_order, y_at):
+                if o:
+                    act(x, y)
+                else:
+                    pl.when(i != 0)(functools.partial(act, x, y))
+            return c
+
+        lax.fori_loop(0, nx, one_row, 0)
+
+    ins = [pltpu.make_async_copy(flux_h, flux, in_sem.at[0]), pltpu.make_async_copy(diff_h, diff, in_sem.at[1])]
+    ins += [
+        pltpu.make_async_copy(r, recs.at[i], in_sem.at[2 + i]) for i, r in enumerate((own_h, src_h, tgt_h, wgt_h))
+    ]
+    for c in ins:
+        c.start()
     bank_copy = pltpu.make_async_copy(bank, bank_v, bank_sem)
     bank_copy.start()
 
-    records = own.shape[1]
+    def greet(x, y):
+        pl.semaphore_signal(barrier, inc=1, device_id=(x, y), device_id_type=MESH)
+
+    each_other(greet)
+
+    ins[0].wait()
+    for f in range(fields):
+        for h in range(2):
+            xs[0, h, f * rows : (f + 1) * rows, :] = flux[f, :, h * LANES : (h + 1) * LANES]
+    lane_c = lane_of((rows, LANES))
+    first = jnp.zeros((rows, LANES), jnp.float32)
+    last = jnp.zeros((rows, LANES), jnp.float32)
+    for f in range(fields):
+        a = flux[f, :, 0:LANES]
+        b = flux[f, :, cols - LANES : cols]
+        first = jnp.where(lane_c == f, pltpu.roll(a, f, 1) if f else a, first)
+        last = jnp.where(lane_c == f, pltpu.roll(b, f + 1, 1), last)
+    col_s[0] = first
+    col_s[1] = last
+    for h in range(2):
+        row_s[0, h] = xs[0, h, pl.ds(0, fields, stride=rows), :]
+        row_s[1, h] = xs[0, h, pl.ds(rows - 1, fields, stride=rows), :]
+
+    ins[1].wait()
+    pl.semaphore_wait(barrier, n - 1)
+
+    def remote(a, b, k, x, y):
+        return pltpu.make_async_remote_copy(
+            src_ref=a, dst_ref=b, send_sem=h_send.at[k], recv_sem=h_recv.at[k],
+            device_id=(x, y), device_id_type=MESH,
+        )
+
+    flux_copies = [
+        remote(row_s.at[0], row_r.at[1], 0, up, gy),
+        remote(row_s.at[1], row_r.at[0], 1, down, gy),
+        remote(col_s.at[0], col_r.at[1], 2, gx, left),
+        remote(col_s.at[1], col_r.at[0], 3, gx, right),
+    ]
+    for c in flux_copies:
+        c.start()
+
+    def halo_copies(base, edge0, edge1, row0, row1, edge, corner, row):
+        low = pl.ds(0, 8)
+        high = pl.ds(orows - 8, 8)
+        return [
+            remote(edge0, edge.at[1], base, gx, left),
+            remote(edge1, edge.at[0], base + 1, gx, right),
+            remote(row0, row.at[1], base + 2, up, gy),
+            remote(row1, row.at[0], base + 3, down, gy),
+            remote(edge0.at[low], corner.at[1, 1], base + 4, up, left),
+            remote(edge0.at[high], corner.at[0, 1], base + 5, down, left),
+            remote(edge1.at[low], corner.at[1, 0], base + 6, up, right),
+            remote(edge1.at[high], corner.at[0, 0], base + 7, down, right),
+        ]
+
+    diff_copies = halo_copies(
+        4, diff, diff, diff.at[pl.ds(0, 8)], diff.at[pl.ds(orows - 8, 8)], d_edge, d_corner, d_row
+    )
+    for c in diff_copies:
+        c.start()
+
+    for c in ins[2:]:
+        c.wait()
+    records = recs.shape[2]
     owner_i = lax.broadcasted_iota(jnp.int32, (n, records), 0)
-    member = own[...] == owner_i
+    member = recs[0] == owner_i
     lower = lax.broadcasted_iota(jnp.int32, (records, records), 0) < lane_of((records, records))
     before = jnp.dot(
         member.astype(jnp.bfloat16), lower.astype(jnp.bfloat16), preferred_element_type=jnp.float32
     )
-    source, target = src[...], tgt[...]
-    code = (wgt[...] * tiles + lax.rem(source, tiles_y) * tiles_x + source // tiles_y).astype(jnp.float32)
+    source, target = recs[1], recs[2]
+    code = (recs[3] * tiles + lax.rem(source, tiles_y) * tiles_x + source // tiles_y).astype(jnp.float32)
     aim = (lax.rem(target, oty) * (fields * otx) + target // oty).astype(jnp.float32)
     lane = lane_of((n, LANES))
     slot_lane = lax.rem(lane, span) // fields
@@ -98,103 +177,26 @@
         meta_s[o] = meta[o : o + 1, :]
     meta_r[me] = meta_s[me]
 
-    for f in range(fields):
-        for h in range(2):
-            xs[0, h, f * rows : (f + 1) * rows, :] = flux[f, :, h * LANES : (h + 1) * LANES]
-    lane_c = lane_of((rows, LANES))
-    first = jnp.zeros((rows, LANES), jnp.float32)
-    last = jnp.zeros((rows, LANES), jnp.float32)
-    for f in range(fields):
-        a = flux[f, :, 0:LANES]
-        b = flux[f, :, cols - LANES : cols]
-        first = jnp.where(lane_c == f, pltpu.roll(a, f, 1) if f else a, first)
-        last = jnp.where(lane_c == f, pltpu.roll(b, f + 1, 1), last)
-    col_s[0] = first
-    col_s[1] = last
-    for h in range(2):
-        row_s[0, h] = xs[0, h, pl.ds(0, fields, stride=rows), :]
-        row_s[1, h] = xs[0, h, pl.ds(rows - 1, fields, stride=rows), :]
-
-    pl.semaphore_wait(barrier, n - 1)
-
-    def remote(a, b, k, x, y):
-        return pltpu.make_async_remote_copy(
-            src_ref=a, dst_ref=b, send_sem=h_send.at[k], recv_sem=h_recv.at[k],
-            device_id=(x, y), device_id_type=MESH,
-        )
-
-    flux_copies = [
-        remote(row_s.at[0], row_r.at[1], 0, up, gy),
-        remote(row_s.at[1], row_r.at[0], 1, down, gy),
-        remote(col_s.at[0], col_r.at[1], 2, gx, left),
-        remote(col_s.at[1], col_r.at[0], 3, gx, right),
-    ]
-    for c in flux_copies:
-        c.start()
-
-    def halo_copies(base, edge0, edge1, row0, row1, edge, corner, row):
-        low = pl.ds(0, 8)
-        high = pl.ds(orows - 8, 8)
-        return [
-            remote(edge0, edge.at[1], base, gx, left),
-            remote(edge1, edge.at[0], base + 1, gx, right),
-            remote(row0, row.at[1], base + 2, up, gy),
-            remote(row1, row.at[0], base + 3, down, gy),
-            remote(edge0.at[low], corner.at[1, 1], base + 4, up, left),
-            remote(edge0.at[high], corner.at[0, 1], base + 5, down, left),
-            remote(edge1.at[low], corner.at[1, 0], base + 6, up, right),
-            remote(edge1.at[high], corner.at[0, 0], base + 7, down, right),
-        ]
-
-    diff_copies = halo_copies(
-        4, diff, diff, diff.at[pl.ds(0, 8)], diff.at[pl.ds(orows - 8, 8)], d_edge, d_corner, d_row
-    )
-    for c in diff_copies:
-        c.start()
-
-    def meta_to(d):
+    def meta_to(x, y):
+        d = x * ny + y
         return pltpu.make_async_remote_copy(
             src_ref=meta_s.at[d], dst_ref=meta_r.at[me], send_sem=m_send.at[d], recv_sem=m_recv.at[me],
-            device_id=(d // ny, lax.rem(d, ny)), device_id_type=MESH,
-        )
-
-    def data_to(d):
+            device_id=(x, y), device_id_type=MESH,
+        )
+
+    def data_to(x, y):
+        d = x * ny + y
         return pltpu.make_async_remote_copy(
             src_ref=sent.at[d], dst_ref=got.at[me], send_sem=a_send.at[d], recv_sem=a_recv.at[me],
-            device_id=(d // ny, lax.rem(d, ny)), device_id_type=MESH,
-        )
-
-    def send_meta(k, c):
-        meta_to(lax.rem(me + k, n)).start()
-        return c
-
-    lax.fori_loop(1, n, send_meta, 0)
-
-    for c in flux_copies:
-        c.wait()
-    row_i = lax.broadcasted_iota(jnp.int32, (rows, LANES), 0)
-    for f in range(fields):
-        halves = [flux[f, :, h * LANES : (h + 1) * LANES] for h in range(2)]
-        ends = (
-            pltpu.roll(col_r[0], LANES - f, 1) if f else col_r[0],
-            pltpu.roll(col_r[1], LANES - 1 - f, 1),
-        )
-        to_right = [pltpu.roll(x, 1, 1) for x in halves]
-        to_left = [pltpu.roll(x, LANES - 1, 1) for x in halves]
-        at_first, at_last = lane_c == 0, lane_c == LANES - 1
-        before_y = [jnp.where(at_first, ends[0], to_right[0]), jnp.where(at_first, to_right[0], to_right[1])]
-        after_y = [jnp.where(at_last, to_left[1], to_left[0]), jnp.where(at_last, ends[1], to_left[1])]
-        for h in range(2):
-            x = halves[h]
-            above = jnp.where(row_i == 0, row_r[0, h, f : f + 1, :], pltpu.roll(x, 1, 0))
-            below = jnp.where(row_i == rows - 1, row_r[1, h, f : f + 1, :], pltpu.roll(x, rows - 1, 0))
-            xs[1, h, f * rows : (f + 1) * rows, :] = (below - above) * 0.5
-            xs[2, h, f * rows : (f + 1) * rows, :] = (after_y[h] - before_y[h]) * 0.5
+            device_id=(x, y), device_id_type=MESH,
+        )
+
+    each_other(lambda x, y: meta_to(x, y).start())
 
     per = LANES // TILE_Y
     halfx = TILE_X // per
     tile_rows = tiles_x * fields
-    for c in range(3):
+    def spread(c):
         for h in range(2):
             for g in range(halfx):
                 parts = [
@@ -213,6 +215,31 @@
                     j = h * per + t
                     xmat[j * tile_rows : (j + 1) * tile_rows, at : at + LANES] = parts[t].astype(jnp.bfloat16)
 
+    spread(0)
+
+    for c in flux_copies:
+        c.wait()
+    row_i = lax.broadcasted_iota(jnp.int32, (rows, LANES), 0)
+    for f in range(fields):
+        halves = [flux[f, :, h * LANES : (h + 1) * LANES] for h in range(2)]
+        ends = (
+            pltpu.roll(col_r[0], LANES - f, 1) if f else col_r[0],
+            pltpu.roll(col_r[1], LANES - 1 - f, 1),
+        )
+        to_right = [pltpu.roll(x, 1, 1) for x in halves]
+        to_left = [pltpu.roll(x, LANES - 1, 1) for x in halves]
+        at_first, at_last = lane_c == 0, lane_c == LANES - 1
+        before_y = [jnp.where(at_first, ends[0], to_right[0]), jnp.where(at_first, to_right[0], to_right[1])]
+        after_y = [jnp.where(at_last, to_left[1], to_left[0]), jnp.where(at_last, ends[1], to_left[1])]
+        for h in range(2):
+            x = halves[h]
+            above = jnp.where(row_i == 0, row_r[0, h, f : f + 1, :], pltpu.roll(x, 1, 0))
+            below = jnp.where(row_i == rows - 1, row_r[1, h, f : f + 1, :], pltpu.roll(x, rows - 1, 0))
+            xs[1, h, f * rows : (f + 1) * rows, :] = (below - above) * 0.5
+            xs[2, h, f * rows : (f + 1) * rows, :] = (after_y[h] - before_y[h]) * 0.5
+
+    spread(1)
+    spread(2)
     bank_copy.wait()
 
     def products(p, c):
@@ -233,13 +260,11 @@
             pair = jnp.concatenate([record(d, s), record(d, s + 1)], axis=0)
             ref[d, s * fields : (s + 2) * fields, :] = pair.astype(jnp.bfloat16)
 
-    def send_data(k, c):
-        d = lax.rem(me + k, n)
-        fill(d, sent)
-        data_to(d).start()
-        return c
-
-    lax.fori_loop(1, n, send_data, 0)
+    def send_data(x, y):
+        fill(x * ny + y, sent)
+        data_to(x, y).start()
+
+    each_other(send_data)
     fill(me, got)
 
     group = max(1, 2 * LANES // span)
@@ -305,6 +330,11 @@
     for c in ocean_copies:
         c.start()
 
+    def settle(x, y):
+        meta_to(x, y).wait_send()
+        data_to(x, y).wait_send()
+
+    each_other(settle)
     for c in diff_copies:
         c.wait()
 
@@ -362,14 +392,6 @@
             x = [x[h] + d[h] * (beside[h] - 4.0 * x[h]) for h in range(2)]
         out[f] = x[0][0:orows, :]
 
-    def settle(k, c):
-        t = lax.rem(me + k, n)
-        meta_to(t).wait_send()
-        data_to(t).wait_send()
-        return c
-
-    lax.fori_loop(1, n, settle, 0)
-
 
 def local(nx, ny, flux, diffusivity, remap_bank, rec_owner, rec_source, rec_target, rec_weight):
     n = nx * ny
@@ -389,9 +411,13 @@
     return pl.pallas_call(
         functools.partial(kernel, nx, ny, cap),
         out_shape=jax.ShapeDtypeStruct((fields, orows, ocols), f32),
-        in_specs=[vm, vm, pl.BlockSpec(memory_space=pl.ANY)] + [vm] * 4,
+        in_specs=[pl.BlockSpec(memory_space=pl.ANY)] * 7,
         out_specs=vm,
         scratch_shapes=[
+            v((fields, rows, cols), f32),
+            v((orows, ocols), f32),
+            v((4, 1, records), jnp.int32),
+            dma((6,)),
             v((nwb, depth, LANES), bf16),
             v((3, 2, (fields + 1) * rows, LANES), f32),
             v((tiles * fields, depth), bf16),
@@ -419,7 +445,7 @@
             dma((20,)), dma((20,)),
         ],
         compiler_params=pltpu.CompilerParams(
-            collective_id=0, has_side_effects=True, vmem_limit_bytes=40 * 1024 * 1024
+            collective_id=0, has_side_effects=True, vmem_limit_bytes=64 * 1024 * 1024 - 128 * 1024
         ),
     )(flux, diffusivity, remap_bank.reshape(nwb, depth, LANES), *flat)
 

time: 47.3 us -> 41 us (0.87)
  local copies, waits for them, and re-layouts: 6.92 us -> 1.57 us
  Pallas kernels: 40.1 us -> 39.2 us
    unnamed x15 -> x1, local copies, waits for them, and re-layouts: 6.92 us -> 1.57 us
    pallas_call x1, Pallas kernels: 40.1 us -> 39.2 us  [local(): pl.pallas_call(functools.partial(kernel, nx, ny, cap), out_shape=jax.Shap...]
where the time goes in v2:
time: 41 us; the launch traced here: 40.8 us
  Pallas kernels  39.2 us (96%)
  local copies, waits for them, and re-layouts  1.57 us (4%)
    pallas_call x1, Pallas kernels, local(): pl.pallas_call(functools.partial(kernel, nx, ny, cap), out_shape=jax.Shap...  39.2 us
    unnamed x1, local copies, waits for them, and re-layouts  1.57 us

profile of v2, /device:TPU:0, one launch (start us, length us, event | category | flops | bytes accessed | tf_op | source)
XLA Modules:
  0.0 40.8 jit_solution(376392955867577358)
XLA Ops:
  0.0 39.2 %shard_map.73 = f32[8,32,128]{2,1,0:T(8,128)} custom-call(f32[8,64,256]{2,1,0:T(8,128)} %flux_h.1, f32[32,128]{1,0:T(8,128)} %diff_h.1, bf16[16,768,128]{2,1,0:T(8,128)(2,1)} %bitcast.5, s32[1,128]{1,0:T(1,128)} %bitcast.6, s32[1,128]{1,0:T(1,128)} %bitcast.7, s32[1,128]{1,0:T(1,128)} %bitcast.8, s32[1,128]{1,0:T(1,128)} %bitcast.9), custom_call_target="tpu_custom_call" | custom-call | tf_op jit(solution)/shard_map/pallas_call | solution.py:411
  39.3 1.6 %copy.9 = f32[8,32,128]{2,1,0:T(8,128)} copy(f32[8,32,128]{2,1,0:T(8,128)} %shard_map.73) | data formatting | bytes 262144

commit v3 on v2

--- a/solution.py
+++ b/solution.py
@@ -42,7 +42,7 @@
     out,
     flux, diff, recs, in_sem,
     bank_v, xs, xmat, prod, table_v, table_s, meta_s, meta_r, sent, got,
-    row_s, row_r, col_s, col_r, d_edge, d_corner, d_row, u, pack_s, u_edge, u_corner, u_row,
+    row_s, row_r, col_s, col_r, d_edge, d_corner, d_row, u, pack_s, u_edge, u_corner, u_row, part_s, part_r,
     bank_sem, table_sem, a_send, a_recv, m_send, m_recv, h_send, h_recv,
 ):
     n = nx * ny
@@ -75,6 +75,15 @@
             return c
 
         lax.fori_loop(0, nx, one_row, 0)
+
+    hy = ny // 2
+    hn = n // 2
+    base = gy // hy * hy
+    other = hy - base
+    mine_j = gy - base
+    place = gx * hy + mine_j
+    j_order = [o for k in range(hy // 2 + 1) for o in sorted({hy // 2 - k, hy // 2 + k}) if o < hy]
+    j_at = [mine_j if o == 0 else lax.rem(mine_j + o, hy) for o in j_order]
 
     ins = [pltpu.make_async_copy(flux_h, flux, in_sem.at[0]), pltpu.make_async_copy(diff_h, diff, in_sem.at[1])]
     ins += [
@@ -175,23 +184,40 @@
     table_copy.start()
     for o in range(n):
         meta_s[o] = meta[o : o + 1, :]
-    meta_r[me] = meta_s[me]
-
-    def meta_to(x, y):
-        d = x * ny + y
+
+    def parties(kind, x, j):
+        owner = x * ny + (base if kind else other) + j
+        return owner, kind * hn + place, (x, base + j)
+
+    def meta_to(kind, x, j):
+        owner, slot, device = parties(kind, x, j)
         return pltpu.make_async_remote_copy(
-            src_ref=meta_s.at[d], dst_ref=meta_r.at[me], send_sem=m_send.at[d], recv_sem=m_recv.at[me],
-            device_id=(x, y), device_id_type=MESH,
+            src_ref=meta_s.at[owner], dst_ref=meta_r.at[slot], send_sem=m_send.at[owner], recv_sem=m_recv.at[slot],
+            device_id=device, device_id_type=MESH,
         )
 
-    def data_to(x, y):
-        d = x * ny + y
+    def data_to(kind, x, j):
+        owner, slot, device = parties(kind, x, j)
         return pltpu.make_async_remote_copy(
-            src_ref=sent.at[d], dst_ref=got.at[me], send_sem=a_send.at[d], recv_sem=a_recv.at[me],
-            device_id=(x, y), device_id_type=MESH,
+            src_ref=sent.at[owner], dst_ref=got.at[slot], send_sem=a_send.at[owner], recv_sem=a_recv.at[slot],
+            device_id=device, device_id_type=MESH,
         )
 
-    each_other(lambda x, y: meta_to(x, y).start())
+    def half_others(act):
+        def one_row(i, c):
+            x = lax.rem(gx + i, nx)
+            for k, j in zip(j_order, j_at):
+                if k:
+                    act(x, j)
+                else:
+                    pl.when(i != 0)(functools.partial(act, x, j))
+            return c
+
+        lax.fori_loop(0, nx, one_row, 0)
+
+    for kind in range(2):
+        meta_r[kind * hn + place] = meta_s[gx * ny + (base if kind else other) + mine_j]
+        half_others(lambda x, j: meta_to(kind, x, j).start())
 
     per = LANES // TILE_Y
     halfx = TILE_X // per
@@ -255,19 +281,22 @@
     def record(d, s):
         return prod[jnp.clip(table_s[d, s], 0, nwb * tiles - 1)]
 
-    def fill(d, ref):
+    def fill(d, ref, at):
         for s in range(0, cap, 2):
             pair = jnp.concatenate([record(d, s), record(d, s + 1)], axis=0)
-            ref[d, s * fields : (s + 2) * fields, :] = pair.astype(jnp.bfloat16)
-
-    def send_data(x, y):
-        fill(x * ny + y, sent)
-        data_to(x, y).start()
-
-    each_other(send_data)
-    fill(me, got)
-
-    group = max(1, 2 * LANES // span)
+            ref[at, s * fields : (s + 2) * fields, :] = pair.astype(jnp.bfloat16)
+
+    for kind in range(2):
+
+        def send_data(x, j):
+            d = parties(kind, x, j)[0]
+            fill(d, sent, d)
+            data_to(kind, x, j).start()
+
+        half_others(send_data)
+        fill(gx * ny + (base if kind else other) + mine_j, got, kind * hn + place)
+
+    group = min(hn, max(1, 2 * LANES // span))
     cells = fields * otx * oty
     shares = LANES // span
     cell_i = lax.broadcasted_iota(jnp.int32, (cells, LANES), 0).astype(jnp.float32)
@@ -277,15 +306,16 @@
         def arrive(i, c):
             s = q * group + i
 
-            @pl.when(s != me)
+            @pl.when(lax.rem(s, hn) != place)
             def _():
+                device = (lax.rem(s, hn) // hy, base + lax.rem(s, hy))
                 pltpu.make_async_remote_copy(
                     src_ref=meta_s.at[s], dst_ref=meta_r.at[s], send_sem=m_send.at[s], recv_sem=m_recv.at[s],
-                    device_id=(s // ny, lax.rem(s, ny)), device_id_type=MESH,
+                    device_id=device, device_id_type=MESH,
                 ).wait_recv()
                 pltpu.make_async_remote_copy(
                     src_ref=sent.at[s], dst_ref=got.at[s], send_sem=a_send.at[s], recv_sem=a_recv.at[s],
-                    device_id=(s // ny, lax.rem(s, ny)), device_id_type=MESH,
+                    device_id=device, device_id_type=MESH,
                 ).wait_recv()
 
             return c
@@ -301,7 +331,13 @@
         data = got[pl.ds(q * group, group)].reshape(group * span, LANES)
         return total + jnp.dot(hot, data, preferred_element_type=jnp.float32)
 
-    total = lax.fori_loop(0, n // group, collect, jnp.zeros((cells, LANES), jnp.float32))
+    empty = jnp.zeros((cells, LANES), jnp.float32)
+    part_s[...] = lax.fori_loop(0, hn // group, collect, empty).astype(jnp.bfloat16)
+    cross = remote(part_s, part_r, 20, gx, other + mine_j)
+    cross.start()
+    total = lax.fori_loop(hn // group, n // group, collect, empty)
+    cross.wait()
+    total = total + part_r[...].astype(jnp.float32)
     high = fields * otx
     parts = block_transpose([total[t * high : (t + 1) * high, :] for t in range(oty)], OTILE_Y)
     for a in range(OTILE_X):
@@ -330,11 +366,13 @@
     for c in ocean_copies:
         c.start()
 
-    def settle(x, y):
-        meta_to(x, y).wait_send()
-        data_to(x, y).wait_send()
-
-    each_other(settle)
+    for kind in range(2):
+
+        def settle(x, j):
+            meta_to(kind, x, j).wait_send()
+            data_to(kind, x, j).wait_send()
+
+        half_others(settle)
     for c in diff_copies:
         c.wait()
 
@@ -440,9 +478,11 @@
             v((2, orows, LANES), f32),
             v((2, 2, 8, LANES), f32),
             v((2, fields * 8, LANES), f32),
+            v((fields * orows * ocols // LANES, LANES), bf16),
+            v((fields * orows * ocols // LANES, LANES), bf16),
             dma, dma,
             dma((n,)), dma((n,)), dma((n,)), dma((n,)),
-            dma((20,)), dma((20,)),
+            dma((21,)), dma((21,)),
         ],
         compiler_params=pltpu.CompilerParams(
             collective_id=0, has_side_effects=True, vmem_limit_bytes=64 * 1024 * 1024 - 128 * 1024

time: 41 us -> 38.3 us (0.934)
  Pallas kernels: 39.2 us -> 36.5 us
    pallas_call x1, Pallas kernels: 39.2 us -> 36.5 us  [local(): pl.pallas_call(functools.partial(kernel, nx, ny, cap), out_shape=jax.Shap...]
where the time goes in v3:
time: 38.3 us; the launch traced here: 38.1 us
  Pallas kernels  36.5 us (95%)
  local copies, waits for them, and re-layouts  1.57 us (4%)
    pallas_call x1, Pallas kernels, local(): pl.pallas_call(functools.partial(kernel, nx, ny, cap), out_shape=jax.Shap...  36.5 us
    unnamed x1, local copies, waits for them, and re-layouts  1.57 us

profile of v3, /device:TPU:0, one launch (start us, length us, event | category | flops | bytes accessed | tf_op | source)
XLA Modules:
  0.0 38.1 jit_solution(10949794069090292078)
XLA Ops:
  0.0 36.5 %shard_map.73 = f32[8,32,128]{2,1,0:T(8,128)} custom-call(f32[8,64,256]{2,1,0:T(8,128)} %flux_h.1, f32[32,128]{1,0:T(8,128)} %diff_h.1, bf16[16,768,128]{2,1,0:T(8,128)(2,1)} %bitcast.5, s32[1,128]{1,0:T(1,128)} %bitcast.6, s32[1,128]{1,0:T(1,128)} %bitcast.7, s32[1,128]{1,0:T(1,128)} %bitcast.8, s32[1,128]{1,0:T(1,128)} %bitcast.9), custom_call_target="tpu_custom_call" | custom-call | tf_op jit(solution)/shard_map/pallas_call | solution.py:449
  36.6 1.6 %copy.9 = f32[8,32,128]{2,1,0:T(8,128)} copy(f32[8,32,128]{2,1,0:T(8,128)} %shard_map.73) | data formatting | bytes 262144

commit v4 on v3

--- a/solution.py
+++ b/solution.py
@@ -42,7 +42,7 @@
     out,
     flux, diff, recs, in_sem,
     bank_v, xs, xmat, prod, table_v, table_s, meta_s, meta_r, sent, got,
-    row_s, row_r, col_s, col_r, d_edge, d_corner, d_row, u, pack_s, u_edge, u_corner, u_row, part_s, part_r,
+    row_s, row_r, col_s, col_r, d_edge, d_corner, d_row, u, pack_s, u_edge, u_corner, u_row, part_s, part_r, hot,
     bank_sem, table_sem, a_send, a_recv, m_send, m_recv, h_send, h_recv,
 ):
     n = nx * ny
@@ -183,23 +183,23 @@
     table_copy = pltpu.make_async_copy(table_v, table_s, table_sem)
     table_copy.start()
     for o in range(n):
-        meta_s[o] = meta[o : o + 1, :]
+        meta_s[o // ny * hy + o % hy, o % ny // hy] = meta[o : o + 1, :]
+    meta_r[place] = meta_s[place]
 
     def parties(kind, x, j):
         owner = x * ny + (base if kind else other) + j
         return owner, kind * hn + place, (x, base + j)
 
-    def meta_to(kind, x, j):
-        owner, slot, device = parties(kind, x, j)
+    def meta_to(x, j):
         return pltpu.make_async_remote_copy(
-            src_ref=meta_s.at[owner], dst_ref=meta_r.at[slot], send_sem=m_send.at[owner], recv_sem=m_recv.at[slot],
-            device_id=device, device_id_type=MESH,
+            src_ref=meta_s.at[x * hy + j], dst_ref=meta_r.at[place], send_sem=m_send, recv_sem=m_recv,
+            device_id=(x, base + j), device_id_type=MESH,
         )
 
     def data_to(kind, x, j):
         owner, slot, device = parties(kind, x, j)
         return pltpu.make_async_remote_copy(
-            src_ref=sent.at[owner], dst_ref=got.at[slot], send_sem=a_send.at[owner], recv_sem=a_recv.at[slot],
+            src_ref=sent.at[owner], dst_ref=got.at[slot], send_sem=a_send, recv_sem=a_recv.at[kind],
             device_id=device, device_id_type=MESH,
         )
 
@@ -215,9 +215,7 @@
 
         lax.fori_loop(0, nx, one_row, 0)
 
-    for kind in range(2):
-        meta_r[kind * hn + place] = meta_s[gx * ny + (base if kind else other) + mine_j]
-        half_others(lambda x, j: meta_to(kind, x, j).start())
+    half_others(lambda x, j: meta_to(x, j).start())
 
     per = LANES // TILE_Y
     halfx = TILE_X // per
@@ -296,46 +294,40 @@
         half_others(send_data)
         fill(gx * ny + (base if kind else other) + mine_j, got, kind * hn + place)
 
-    group = min(hn, max(1, 2 * LANES // span))
     cells = fields * otx * oty
     shares = LANES // span
+    depth = hn * span
     cell_i = lax.broadcasted_iota(jnp.int32, (cells, LANES), 0).astype(jnp.float32)
     part_lane = lane_of((1, LANES)) // span
-
-    def collect(q, total):
-        def arrive(i, c):
-            s = q * group + i
-
-            @pl.when(lax.rem(s, hn) != place)
-            def _():
-                device = (lax.rem(s, hn) // hy, base + lax.rem(s, hy))
-                pltpu.make_async_remote_copy(
-                    src_ref=meta_s.at[s], dst_ref=meta_r.at[s], send_sem=m_send.at[s], recv_sem=m_recv.at[s],
-                    device_id=device, device_id_type=MESH,
-                ).wait_recv()
-                pltpu.make_async_remote_copy(
-                    src_ref=sent.at[s], dst_ref=got.at[s], send_sem=a_send.at[s], recv_sem=a_recv.at[s],
-                    device_id=device, device_id_type=MESH,
-                ).wait_recv()
-
-            return c
-
-        lax.fori_loop(0, group, arrive, 0)
-        hots = []
-        for b in range(group // shares):
-            aims = meta_r[q * group + b * shares]
+    mine_half = gy // hy
+
+    def whole(src_ref, dst_ref, send_sem, recv_sem):
+        return pltpu.make_async_remote_copy(
+            src_ref=src_ref, dst_ref=dst_ref, send_sem=send_sem, recv_sem=recv_sem,
+            device_id=(gx, other + mine_j), device_id_type=MESH,
+        )
+
+    meta_all = whole(meta_s.at[pl.ds(0, hn - 1)], meta_r.at[pl.ds(0, hn - 1)], m_send, m_recv)
+    meta_all.wait_recv()
+    for kind in range(2):
+        row = mine_half if kind else 1 - mine_half
+        for b in range(depth // LANES):
+            aims = meta_r[b * shares, row]
             for i in range(1, shares):
-                aims = jnp.where(part_lane == i, meta_r[q * group + b * shares + i], aims)
-            hots.append(jnp.where(cell_i == aims, 1.0, 0.0).astype(jnp.bfloat16))
-        hot = jnp.concatenate(hots, axis=1)
-        data = got[pl.ds(q * group, group)].reshape(group * span, LANES)
-        return total + jnp.dot(hot, data, preferred_element_type=jnp.float32)
-
-    empty = jnp.zeros((cells, LANES), jnp.float32)
-    part_s[...] = lax.fori_loop(0, hn // group, collect, empty).astype(jnp.bfloat16)
+                aims = jnp.where(part_lane == i, meta_r[b * shares + i, row], aims)
+            at = kind * depth + b * LANES
+            hot[:, at : at + LANES] = jnp.where(cell_i == aims, 1.0, 0.0).astype(jnp.bfloat16)
+
+    def collect(kind):
+        ref = got.at[pl.ds(kind * hn, hn - 1)]
+        whole(ref, ref, a_send, a_recv.at[kind]).wait_recv()
+        data = got[kind * hn : (kind + 1) * hn].reshape(depth, LANES)
+        return jnp.dot(hot[:, kind * depth : (kind + 1) * depth], data, preferred_element_type=jnp.float32)
+
+    part_s[...] = collect(0).astype(jnp.bfloat16)
     cross = remote(part_s, part_r, 20, gx, other + mine_j)
     cross.start()
-    total = lax.fori_loop(hn // group, n // group, collect, empty)
+    total = collect(1)
     cross.wait()
     total = total + part_r[...].astype(jnp.float32)
     high = fields * otx
@@ -366,13 +358,9 @@
     for c in ocean_copies:
         c.start()
 
-    for kind in range(2):
-
-        def settle(x, j):
-            meta_to(kind, x, j).wait_send()
-            data_to(kind, x, j).wait_send()
-
-        half_others(settle)
+    meta_all.wait_send()
+    ref = sent.at[pl.ds(0, 2 * (hn - 1))]
+    whole(ref, ref, a_send, a_recv.at[0]).wait_send()
     for c in diff_copies:
         c.wait()
 
@@ -407,28 +395,35 @@
     lane_e = lane_of((ext, LANES))
     side_ok = jnp.concatenate([col_ok, both_ok], axis=0)
     at_first, at_last = lane_e == 0, lane_e == LANES - 1
-    for f in range(fields):
+    def opened(f):
         shift = f * SWEEPS
         tail = jnp.where(tail_row, u_row[1, f * 8 : f * 8 + 8, :], u_row[0, f * 8 : f * 8 + 8, :]) * row_ok
         rolled = (
             (pltpu.roll(side[1], LANES - shift, 1), pltpu.roll(side[0], shift, 1)) if f else (side[1], side[0])
         )
-        x = [
+        return [
             jnp.concatenate([u[f * orows : (f + 1) * orows, :], tail], axis=0),
             jnp.where(lane_e < LANES // 2, rolled[0], rolled[1]) * side_ok,
         ]
+
+    def swept(x):
+        to_right = [pltpu.roll(v, 1, 1) for v in x]
+        to_left = [pltpu.roll(v, LANES - 1, 1) for v in x]
+        beside = [
+            jnp.where(at_first, to_right[1 - h], to_right[h])
+            + jnp.where(at_last, to_left[1 - h], to_left[h])
+            + pltpu.roll(x[h], 1, 0)
+            + pltpu.roll(x[h], ext - 1, 0)
+            for h in range(2)
+        ]
+        return [x[h] + d[h] * (beside[h] - 4.0 * x[h]) for h in range(2)]
+
+    for f in range(0, fields, 2):
+        pair = [opened(f), opened(f + 1)]
         for sweep in range(SWEEPS):
-            to_right = [pltpu.roll(v, 1, 1) for v in x]
-            to_left = [pltpu.roll(v, LANES - 1, 1) for v in x]
-            beside = [
-                jnp.where(at_first, to_right[1 - h], to_right[h])
-                + jnp.where(at_last, to_left[1 - h], to_left[h])
-                + pltpu.roll(x[h], 1, 0)
-                + pltpu.roll(x[h], ext - 1, 0)
-                for h in range(2)
-            ]
-            x = [x[h] + d[h] * (beside[h] - 4.0 * x[h]) for h in range(2)]
-        out[f] = x[0][0:orows, :]
+            pair = [swept(x) for x in pair]
+        for i, x in enumerate(pair):
+            out[f + i] = x[0][0:orows, :]
 
 
 def local(nx, ny, flux, diffusivity, remap_bank, rec_owner, rec_source, rec_target, rec_weight):
@@ -462,8 +457,8 @@
             v((nwb * tiles, fields, LANES), f32),
             v((n, LANES), jnp.int32),
             pltpu.SMEM((n, LANES), jnp.int32),
-            v((n, 1, LANES), f32),
-            v((n, 1, LANES), f32),
+            v((n // 2, 2, 1, LANES), f32),
+            v((n // 2, 2, 1, LANES), f32),
             v((n, span, LANES), bf16),
             v((n, span, LANES), bf16),
             v((2, 2, fields, LANES), f32),
@@ -480,8 +475,9 @@
             v((2, fields * 8, LANES), f32),
             v((fields * orows * ocols // LANES, LANES), bf16),
             v((fields * orows * ocols // LANES, LANES), bf16),
+            v((fields * orows * ocols // LANES, n * span), bf16),
             dma, dma,
-            dma((n,)), dma((n,)), dma((n,)), dma((n,)),
+            dma, dma((2,)), dma, dma,
             dma((21,)), dma((21,)),
         ],
         compiler_params=pltpu.CompilerParams(

time: 38.3 us -> 36.3 us (0.948)
  Pallas kernels: 36.5 us -> 34.6 us
    pallas_call x1, Pallas kernels: 36.5 us -> 34.6 us  [local(): pl.pallas_call(functools.partial(kernel, nx, ny, cap), out_shape=jax.Shap...]
where the time goes in v4:
time: 36.3 us; the launch traced here: 36.2 us
  Pallas kernels  34.6 us (95%)
  local copies, waits for them, and re-layouts  1.57 us (4%)
    pallas_call x1, Pallas kernels, local(): pl.pallas_call(functools.partial(kernel, nx, ny, cap), out_shape=jax.Shap...  34.6 us
    unnamed x1, local copies, waits for them, and re-layouts  1.57 us

profile of v4, /device:TPU:0, one launch (start us, length us, event | category | flops | bytes accessed | tf_op | source)
XLA Modules:
  0.0 36.2 jit_solution(312738212053586581)
XLA Ops:
  0.0 34.6 %shard_map.73 = f32[8,32,128]{2,1,0:T(8,128)} custom-call(f32[8,64,256]{2,1,0:T(8,128)} %flux_h.1, f32[32,128]{1,0:T(8,128)} %diff_h.1, bf16[16,768,128]{2,1,0:T(8,128)(2,1)} %bitcast.5, s32[1,128]{1,0:T(1,128)} %bitcast.6, s32[1,128]{1,0:T(1,128)} %bitcast.7, s32[1,128]{1,0:T(1,128)} %bitcast.8, s32[1,128]{1,0:T(1,128)} %bitcast.9), custom_call_target="tpu_custom_call" | custom-call | tf_op jit(solution)/shard_map/pallas_call | solution.py:444
  34.6 1.6 %copy.9 = f32[8,32,128]{2,1,0:T(8,128)} copy(f32[8,32,128]{2,1,0:T(8,128)} %shard_map.73) | data formatting | bytes 262144

commit v5 on v4

--- a/solution.py
+++ b/solution.py
@@ -39,7 +39,7 @@
 def kernel(
     nx, ny, cap,
     flux_h, diff_h, bank, own_h, src_h, tgt_h, wgt_h,
-    out,
+    out, last_step,
     flux, diff, recs, in_sem,
     bank_v, xs, xmat, prod, table_v, table_s, meta_s, meta_r, sent, got,
     row_s, row_r, col_s, col_r, d_edge, d_corner, d_row, u, pack_s, u_edge, u_corner, u_row, part_s, part_r, hot,
@@ -220,50 +220,52 @@
     per = LANES // TILE_Y
     halfx = TILE_X // per
     tile_rows = tiles_x * fields
-    def spread(c):
-        for h in range(2):
-            for g in range(halfx):
-                parts = [
-                    jnp.concatenate(
-                        [
-                            xs[c, h, pl.ds(t * TILE_X + g * per + a, fields, stride=rows), :]
-                            for t in range(tiles_x)
-                        ],
-                        axis=0,
-                    )
-                    for a in range(per)
-                ]
-                parts = block_transpose(parts, TILE_Y)
-                at = (c * halfx + g) * LANES
-                for t in range(per):
-                    j = h * per + t
-                    xmat[j * tile_rows : (j + 1) * tile_rows, at : at + LANES] = parts[t].astype(jnp.bfloat16)
-
-    spread(0)
+
+    def spread(ch, carry):
+        c, h = ch // 2, lax.rem(ch, 2)
+        for g in range(halfx):
+            parts = [
+                jnp.concatenate(
+                    [
+                        xs[c, h, pl.ds(t * TILE_X + g * per + a, fields, stride=rows), :]
+                        for t in range(tiles_x)
+                    ],
+                    axis=0,
+                )
+                for a in range(per)
+            ]
+            parts = block_transpose(parts, TILE_Y)
+            at = pl.ds(pl.multiple_of((c * halfx + g) * LANES, LANES), LANES)
+            for t in range(per):
+                row = pl.ds(pl.multiple_of((h * per + t) * tile_rows, tile_rows), tile_rows)
+                xmat[row, at] = parts[t].astype(jnp.bfloat16)
+        return carry
+
+    lax.fori_loop(0, 2, spread, 0)
 
     for c in flux_copies:
         c.wait()
     row_i = lax.broadcasted_iota(jnp.int32, (rows, LANES), 0)
-    for f in range(fields):
+    at_first, at_last = lane_c == 0, lane_c == LANES - 1
+
+    def slopes(f, carry):
         halves = [flux[f, :, h * LANES : (h + 1) * LANES] for h in range(2)]
-        ends = (
-            pltpu.roll(col_r[0], LANES - f, 1) if f else col_r[0],
-            pltpu.roll(col_r[1], LANES - 1 - f, 1),
-        )
+        ends = (pltpu.roll(col_r[0], lax.rem(LANES - f, LANES), 1), pltpu.roll(col_r[1], LANES - 1 - f, 1))
         to_right = [pltpu.roll(x, 1, 1) for x in halves]
         to_left = [pltpu.roll(x, LANES - 1, 1) for x in halves]
-        at_first, at_last = lane_c == 0, lane_c == LANES - 1
         before_y = [jnp.where(at_first, ends[0], to_right[0]), jnp.where(at_first, to_right[0], to_right[1])]
         after_y = [jnp.where(at_last, to_left[1], to_left[0]), jnp.where(at_last, ends[1], to_left[1])]
+        at = pl.ds(pl.multiple_of(f * rows, rows), rows)
         for h in range(2):
             x = halves[h]
-            above = jnp.where(row_i == 0, row_r[0, h, f : f + 1, :], pltpu.roll(x, 1, 0))
-            below = jnp.where(row_i == rows - 1, row_r[1, h, f : f + 1, :], pltpu.roll(x, rows - 1, 0))
-            xs[1, h, f * rows : (f + 1) * rows, :] = (below - above) * 0.5
-            xs[2, h, f * rows : (f + 1) * rows, :] = (after_y[h] - before_y[h]) * 0.5
-
-    spread(1)
-    spread(2)
+            above = jnp.where(row_i == 0, row_r[0, h, pl.ds(f, 1), :], pltpu.roll(x, 1, 0))
+            below = jnp.where(row_i == rows - 1, row_r[1, h, pl.ds(f, 1), :], pltpu.roll(x, rows - 1, 0))
+            xs[1, h, at, :] = (below - above) * 0.5
+            xs[2, h, at, :] = (after_y[h] - before_y[h]) * 0.5
+        return carry
+
+    lax.fori_loop(0, fields, slopes, 0)
+    lax.fori_loop(2, 6, spread, 0)
     bank_copy.wait()
 
     def products(p, c):
@@ -396,17 +398,16 @@
     side_ok = jnp.concatenate([col_ok, both_ok], axis=0)
     at_first, at_last = lane_e == 0, lane_e == LANES - 1
     def opened(f):
+        at = pl.ds(pl.multiple_of(f * 8, 8), 8)
+        tail = jnp.where(tail_row, u_row[1, at, :], u_row[0, at, :]) * row_ok
         shift = f * SWEEPS
-        tail = jnp.where(tail_row, u_row[1, f * 8 : f * 8 + 8, :], u_row[0, f * 8 : f * 8 + 8, :]) * row_ok
-        rolled = (
-            (pltpu.roll(side[1], LANES - shift, 1), pltpu.roll(side[0], shift, 1)) if f else (side[1], side[0])
-        )
+        rolled = (pltpu.roll(side[1], lax.rem(LANES - shift, LANES), 1), pltpu.roll(side[0], shift, 1))
         return [
-            jnp.concatenate([u[f * orows : (f + 1) * orows, :], tail], axis=0),
+            jnp.concatenate([u[pl.ds(pl.multiple_of(f * orows, orows), orows), :], tail], axis=0),
             jnp.where(lane_e < LANES // 2, rolled[0], rolled[1]) * side_ok,
         ]
 
-    def swept(x):
+    def change(x):
         to_right = [pltpu.roll(v, 1, 1) for v in x]
         to_left = [pltpu.roll(v, LANES - 1, 1) for v in x]
         beside = [
@@ -416,14 +417,19 @@
             + pltpu.roll(x[h], ext - 1, 0)
             for h in range(2)
         ]
-        return [x[h] + d[h] * (beside[h] - 4.0 * x[h]) for h in range(2)]
-
-    for f in range(0, fields, 2):
-        pair = [opened(f), opened(f + 1)]
-        for sweep in range(SWEEPS):
-            pair = [swept(x) for x in pair]
+        return [d[h] * (beside[h] - 4.0 * x[h]) for h in range(2)]
+
+    def sweeps(k, carry):
+        pair = [opened(2 * k), opened(2 * k + 1)]
+        for sweep in range(SWEEPS - 1):
+            steps = [change(x) for x in pair]
+            pair = [[x[h] + y[h] for h in range(2)] for x, y in zip(pair, steps)]
         for i, x in enumerate(pair):
-            out[f + i] = x[0][0:orows, :]
+            out[2 * k + i] = x[0][0:orows, :]
+            last_step[2 * k + i] = change(x)[0][0:orows, :]
+        return carry
+
+    lax.fori_loop(0, fields // 2, sweeps, 0)
 
 
 def local(nx, ny, flux, diffusivity, remap_bank, rec_owner, rec_source, rec_target, rec_weight):
@@ -441,11 +447,11 @@
     dma = pltpu.SemaphoreType.DMA
     vm = pl.BlockSpec(memory_space=pltpu.VMEM)
     flat = [x.reshape(1, records) for x in (rec_owner, rec_source, rec_target, rec_weight)]
-    return pl.pallas_call(
+    state, last_step = pl.pallas_call(
         functools.partial(kernel, nx, ny, cap),
-        out_shape=jax.ShapeDtypeStruct((fields, orows, ocols), f32),
+        out_shape=[jax.ShapeDtypeStruct((fields, orows, ocols), f32)] * 2,
         in_specs=[pl.BlockSpec(memory_space=pl.ANY)] * 7,
-        out_specs=vm,
+        out_specs=[vm, vm],
         scratch_shapes=[
             v((fields, rows, cols), f32),
             v((orows, ocols), f32),
@@ -484,6 +490,7 @@
             collective_id=0, has_side_effects=True, vmem_limit_bytes=64 * 1024 * 1024 - 128 * 1024
         ),
     )(flux, diffusivity, remap_bank.reshape(nwb, depth, LANES), *flat)
+    return state + last_step
 
 
 def solution(mesh):

time: 36.3 us -> 37.3 us (1.028)
  other arithmetic: 0 us -> 1.64 us
  local copies, waits for them, and re-layouts: 1.57 us -> 0 us
  Pallas kernels: 34.6 us -> 35.5 us
    add x0 -> x1, other arithmetic: none -> 1.64 us  [local(): return state + last_step]
    unnamed x1 -> x0, local copies, waits for them, and re-layouts: 1.57 us -> none
    pallas_call x1, Pallas kernels: 34.6 us -> 35.5 us  [local(): pl.pallas_call(functools.partial(kernel, nx, ny, cap), out_shape=[jax.Sha...]
where the time goes in v5:
time: 37.3 us; the launch traced here: 37.1 us
  Pallas kernels  35.5 us (95%)
  other arithmetic  1.64 us (4%)
    pallas_call x1, Pallas kernels, local(): pl.pallas_call(functools.partial(kernel, nx, ny, cap), out_shape=[jax.Sha...  35.5 us
    add x1, other arithmetic, local(): return state + last_step  1.64 us

profile of v5, /device:TPU:0, one launch (start us, length us, event | category | flops | bytes accessed | tf_op | source)
XLA Modules:
  0.0 37.1 jit_solution(1442801353276006623)
XLA Ops:
  0.0 35.5 %shard_map.73 = (f32[8,32,128]{2,1,0:T(8,128)}, f32[8,32,128]{2,1,0:T(8,128)}) custom-call(f32[8,64,256]{2,1,0:T(8,128)} %flux_h.1, f32[32,128]{1,0:T(8,128)} %diff_h.1, bf16[16,768,128]{2,1,0:T(8,128)(2,1)} %bitcast.5, s32[1,128]{1,0:T(1,128)} %bitcast.6, s32[1,128]{1,0:T(1,128)} %bitcast.7, s32[1,128]{1,0:T(1,128)} %bitcast.8, s32[1,128]{1,0:T(1,128)} %bitcast.9), custom_call_target="tpu_custom_call" | custom-call | tf_op jit(solution)/shard_map/pallas_call | solution.py:450
  35.5 1.6 %add.3 = f32[8,32,128]{2,1,0:T(8,128)} add(f32[8,32,128]{2,1,0:T(8,128)} %get-tuple-element.7, f32[8,32,128]{2,1,0:T(8,128)} %get-tuple-element.8) | non-fusion elementwise | flops 32768 | bytes 393216 | tf_op jit(solution)/shard_map/add | solution.py:493

commit v6 on v4

--- a/solution.py
+++ b/solution.py
@@ -61,21 +61,6 @@
 
     barrier = pltpu.get_barrier_semaphore()
 
-    y_order = [o for k in range(ny // 2 + 1) for o in sorted({ny // 2 - k, ny // 2 + k}) if o < ny]
-    y_at = [gy if o == 0 else lax.rem(gy + o, ny) for o in y_order]
-
-    def each_other(act):
-        def one_row(i, c):
-            x = lax.rem(gx + i, nx)
-            for o, y in zip(y_order, y_at):
-                if o:
-                    act(x, y)
-                else:
-                    pl.when(i != 0)(functools.partial(act, x, y))
-            return c
-
-        lax.fori_loop(0, nx, one_row, 0)
-
     hy = ny // 2
     hn = n // 2
     base = gy // hy * hy
@@ -85,21 +70,48 @@
     j_order = [o for k in range(hy // 2 + 1) for o in sorted({hy // 2 - k, hy // 2 + k}) if o < hy]
     j_at = [mine_j if o == 0 else lax.rem(mine_j + o, hy) for o in j_order]
 
-    ins = [pltpu.make_async_copy(flux_h, flux, in_sem.at[0]), pltpu.make_async_copy(diff_h, diff, in_sem.at[1])]
-    ins += [
-        pltpu.make_async_copy(r, recs.at[i], in_sem.at[2 + i]) for i, r in enumerate((own_h, src_h, tgt_h, wgt_h))
+    def half_others(act):
+        def one_row(i, c):
+            x = lax.rem(gx + i, nx)
+            for k, j in zip(j_order, j_at):
+                if k:
+                    act(x, j)
+                else:
+                    pl.when(i != 0)(functools.partial(act, x, j))
+            return c
+
+        lax.fori_loop(0, nx, one_row, 0)
+
+    quarter = fields // 4
+    flux_ins = [
+        pltpu.make_async_copy(flux_h.at[pl.ds(i * quarter, quarter)], flux.at[pl.ds(i * quarter, quarter)], in_sem.at[5 + i])
+        for i in range(4)
     ]
-    for c in ins:
+    ins = [
+        pltpu.make_async_copy(r, recs.at[i], in_sem.at[i]) for i, r in enumerate((own_h, src_h, tgt_h, wgt_h))
+    ]
+    diff_in = pltpu.make_async_copy(diff_h, diff, in_sem.at[4])
+    for c in flux_ins + ins + [diff_in]:
         c.start()
     bank_copy = pltpu.make_async_copy(bank, bank_v, bank_sem)
-    bank_copy.start()
 
     def greet(x, y):
         pl.semaphore_signal(barrier, inc=1, device_id=(x, y), device_id_type=MESH)
 
-    each_other(greet)
-
-    ins[0].wait()
+    greet(gx, other + mine_j)
+    for y, edge in ((left, 0), (right, hy - 1)):
+
+        @pl.when(mine_j == edge)
+        def _():
+            for x in (up, gx, down):
+                greet(x, y)
+
+    half_others(lambda x, j: greet(x, base + j))
+    beside_others = 3 * (mine_j == 0).astype(jnp.int32) + 3 * (mine_j == hy - 1).astype(jnp.int32)
+
+    for c in flux_ins:
+        c.wait()
+    bank_copy.start()
     for f in range(fields):
         for h in range(2):
             xs[0, h, f * rows : (f + 1) * rows, :] = flux[f, :, h * LANES : (h + 1) * LANES]
@@ -117,8 +129,7 @@
         row_s[0, h] = xs[0, h, pl.ds(0, fields, stride=rows), :]
         row_s[1, h] = xs[0, h, pl.ds(rows - 1, fields, stride=rows), :]
 
-    ins[1].wait()
-    pl.semaphore_wait(barrier, n - 1)
+    pl.semaphore_wait(barrier, hn + beside_others)
 
     def remote(a, b, k, x, y):
         return pltpu.make_async_remote_copy(
@@ -149,13 +160,7 @@
             remote(edge1.at[high], corner.at[0, 0], base + 7, down, right),
         ]
 
-    diff_copies = halo_copies(
-        4, diff, diff, diff.at[pl.ds(0, 8)], diff.at[pl.ds(orows - 8, 8)], d_edge, d_corner, d_row
-    )
-    for c in diff_copies:
-        c.start()
-
-    for c in ins[2:]:
+    for c in ins:
         c.wait()
     records = recs.shape[2]
     owner_i = lax.broadcasted_iota(jnp.int32, (n, records), 0)
@@ -203,18 +208,6 @@
             device_id=device, device_id_type=MESH,
         )
 
-    def half_others(act):
-        def one_row(i, c):
-            x = lax.rem(gx + i, nx)
-            for k, j in zip(j_order, j_at):
-                if k:
-                    act(x, j)
-                else:
-                    pl.when(i != 0)(functools.partial(act, x, j))
-            return c
-
-        lax.fori_loop(0, nx, one_row, 0)
-
     half_others(lambda x, j: meta_to(x, j).start())
 
     per = LANES // TILE_Y
@@ -294,6 +287,13 @@
         half_others(send_data)
         fill(gx * ny + (base if kind else other) + mine_j, got, kind * hn + place)
 
+    diff_in.wait()
+    diff_copies = halo_copies(
+        4, diff, diff, diff.at[pl.ds(0, 8)], diff.at[pl.ds(orows - 8, 8)], d_edge, d_corner, d_row
+    )
+    for c in diff_copies:
+        c.start()
+
     cells = fields * otx * oty
     shares = LANES // span
     depth = hn * span
@@ -336,17 +336,9 @@
         u[pl.ds(a, high, stride=OTILE_X), :] = parts[a]
 
     lane_o = lane_of((orows, LANES))
-    packed = [jnp.zeros((orows, LANES), jnp.float32) for _ in range(2)]
     for f in range(fields):
-        block = u[f * orows : (f + 1) * orows, :]
-        shift = f * SWEEPS
-        rolled = (pltpu.roll(block, shift, 1), pltpu.roll(block, LANES - shift, 1)) if f else (block, block)
-        mine = (lane_o // SWEEPS == f, (LANES - 1 - lane_o) // SWEEPS == f)
-        packed = [jnp.where(mine[e], rolled[e], packed[e]) for e in range(2)]
-        pack_s[2, f * 8 : f * 8 + 8, :] = block[0:8]
-        pack_s[3, f * 8 : f * 8 + 8, :] = block[orows - 8 : orows]
-    pack_s[0, 0:orows, :] = packed[0]
-    pack_s[1, 0:orows, :] = packed[1]
+        pack_s[2, f * 8 : f * 8 + 8, :] = u[f * orows : f * orows + 8, :]
+        pack_s[3, f * 8 : f * 8 + 8, :] = u[(f + 1) * orows - 8 : (f + 1) * orows, :]
     ocean_copies = halo_copies(
         12,
         pack_s.at[0, pl.ds(0, orows)],
@@ -355,7 +347,18 @@
         pack_s.at[3, pl.ds(0, fields * 8)],
         u_edge, u_corner, u_row,
     )
-    for c in ocean_copies:
+    for c in ocean_copies[2:4]:
+        c.start()
+    packed = [jnp.zeros((orows, LANES), jnp.float32) for _ in range(2)]
+    for f in range(fields):
+        block = u[f * orows : (f + 1) * orows, :]
+        shift = f * SWEEPS
+        rolled = (pltpu.roll(block, shift, 1), pltpu.roll(block, LANES - shift, 1)) if f else (block, block)
+        mine = (lane_o // SWEEPS == f, (LANES - 1 - lane_o) // SWEEPS == f)
+        packed = [jnp.where(mine[e], rolled[e], packed[e]) for e in range(2)]
+    pack_s[0, 0:orows, :] = packed[0]
+    pack_s[1, 0:orows, :] = packed[1]
+    for c in ocean_copies[4:] + ocean_copies[:2]:
         c.start()
 
     meta_all.wait_send()
@@ -450,7 +453,7 @@
             v((fields, rows, cols), f32),
             v((orows, ocols), f32),
             v((4, 1, records), jnp.int32),
-            dma((6,)),
+            dma((9,)),
             v((nwb, depth, LANES), bf16),
             v((3, 2, (fields + 1) * rows, LANES), f32),
             v((tiles * fields, depth), bf16),

time: 36.3 us -> 35.3 us (0.972)
  Pallas kernels: 34.6 us -> 33.5 us
    pallas_call x1, Pallas kernels: 34.6 us -> 33.5 us  [local(): pl.pallas_call(functools.partial(kernel, nx, ny, cap), out_shape=jax.Shap...]
where the time goes in v6:
time: 35.3 us; the launch traced here: 35.1 us
  Pallas kernels  33.5 us (95%)
  local copies, waits for them, and re-layouts  1.57 us (4%)
    pallas_call x1, Pallas kernels, local(): pl.pallas_call(functools.partial(kernel, nx, ny, cap), out_shape=jax.Shap...  33.5 us
    unnamed x1, local copies, waits for them, and re-layouts  1.57 us

profile of v6, /device:TPU:0, one launch (start us, length us, event | category | flops | bytes accessed | tf_op | source)
XLA Modules:
  0.0 35.1 jit_solution(17600259733322038522)
XLA Ops:
  0.0 33.5 %shard_map.73 = f32[8,32,128]{2,1,0:T(8,128)} custom-call(f32[8,64,256]{2,1,0:T(8,128)} %flux_h.1, f32[32,128]{1,0:T(8,128)} %diff_h.1, bf16[16,768,128]{2,1,0:T(8,128)(2,1)} %bitcast.5, s32[1,128]{1,0:T(1,128)} %bitcast.6, s32[1,128]{1,0:T(1,128)} %bitcast.7, s32[1,128]{1,0:T(1,128)} %bitcast.8, s32[1,128]{1,0:T(1,128)} %bitcast.9), custom_call_target="tpu_custom_call" | custom-call | tf_op jit(solution)/shard_map/pallas_call | solution.py:447
  33.6 1.6 %copy.9 = f32[8,32,128]{2,1,0:T(8,128)} copy(f32[8,32,128]{2,1,0:T(8,128)} %shard_map.73) | data formatting | bytes 262144

commit v7 on v6

--- a/solution.py
+++ b/solution.py
@@ -47,7 +47,7 @@
 ):
     n = nx * ny
     fields, rows, cols = flux.shape
-    nwb = bank.shape[0]
+    nwb = 2 * bank.shape[0]
     tiles_x, tiles_y = rows // TILE_X, cols // TILE_Y
     tiles = tiles_x * tiles_y
     orows = diff.shape[0]
@@ -93,7 +93,9 @@
     diff_in = pltpu.make_async_copy(diff_h, diff, in_sem.at[4])
     for c in flux_ins + ins + [diff_in]:
         c.start()
-    bank_copy = pltpu.make_async_copy(bank, bank_v, bank_sem)
+    bank_copies = [
+        pltpu.make_async_copy(bank.at[:, i], bank_v.at[:, :, pl.ds(i * LANES, LANES)], bank_sem.at[i]) for i in range(2)
+    ]
 
     def greet(x, y):
         pl.semaphore_signal(barrier, inc=1, device_id=(x, y), device_id_type=MESH)
@@ -111,7 +113,8 @@
 
     for c in flux_ins:
         c.wait()
-    bank_copy.start()
+    for c in bank_copies:
+        c.start()
     for f in range(fields):
         for h in range(2):
             xs[0, h, f * rows : (f + 1) * rows, :] = flux[f, :, h * LANES : (h + 1) * LANES]
@@ -257,11 +260,11 @@
 
     spread(1)
     spread(2)
-    bank_copy.wait()
+    for c in bank_copies:
+        c.wait()
 
     def products(p, c):
-        pair = jnp.concatenate([bank_v[2 * p], bank_v[2 * p + 1]], axis=1)
-        got_pair = jnp.dot(xmat[...], pair, preferred_element_type=jnp.float32)
+        got_pair = jnp.dot(xmat[...], bank_v[p], preferred_element_type=jnp.float32)
         prod[pl.ds(2 * p * tiles, tiles)] = got_pair[:, :LANES].reshape(tiles, fields, LANES)
         prod[pl.ds((2 * p + 1) * tiles, tiles)] = got_pair[:, LANES:].reshape(tiles, fields, LANES)
         return c
@@ -421,11 +424,11 @@
         ]
         return [x[h] + d[h] * (beside[h] - 4.0 * x[h]) for h in range(2)]
 
-    for f in range(0, fields, 2):
-        pair = [opened(f), opened(f + 1)]
+    for f in range(0, fields, 4):
+        some = [opened(f + i) for i in range(4)]
         for sweep in range(SWEEPS):
-            pair = [swept(x) for x in pair]
-        for i, x in enumerate(pair):
+            some = [swept(x) for x in some]
+        for i, x in enumerate(some):
             out[f + i] = x[0][0:orows, :]
 
 
@@ -454,7 +457,7 @@
             v((orows, ocols), f32),
             v((4, 1, records), jnp.int32),
             dma((9,)),
-            v((nwb, depth, LANES), bf16),
+            v((nwb // 2, depth, 2 * LANES), bf16),
             v((3, 2, (fields + 1) * rows, LANES), f32),
             v((tiles * fields, depth), bf16),
             v((nwb * tiles, fields, LANES), f32),
@@ -479,14 +482,14 @@
             v((fields * orows * ocols // LANES, LANES), bf16),
             v((fields * orows * ocols // LANES, LANES), bf16),
             v((fields * orows * ocols // LANES, n * span), bf16),
-            dma, dma,
+            dma((2,)), dma,
             dma, dma((2,)), dma, dma,
             dma((21,)), dma((21,)),
         ],
         compiler_params=pltpu.CompilerParams(
             collective_id=0, has_side_effects=True, vmem_limit_bytes=64 * 1024 * 1024 - 128 * 1024
         ),
-    )(flux, diffusivity, remap_bank.reshape(nwb, depth, LANES), *flat)
+    )(flux, diffusivity, remap_bank.reshape(nwb // 2, 2, depth, LANES), *flat)
 
 
 def solution(mesh):

time: 35.3 us -> 34.8 us (0.986)
  Pallas kernels: 33.5 us -> 33.1 us
    pallas_call x1, Pallas kernels: 33.5 us -> 33.1 us  [local(): pl.pallas_call(functools.partial(kernel, nx, ny, cap), out_shape=jax.Shap...]
where the time goes in v7:
time: 34.8 us; the launch traced here: 34.6 us
  Pallas kernels  33.1 us (95%)
  local copies, waits for them, and re-layouts  1.57 us (5%)
    pallas_call x1, Pallas kernels, local(): pl.pallas_call(functools.partial(kernel, nx, ny, cap), out_shape=jax.Shap...  33.1 us
    unnamed x1, local copies, waits for them, and re-layouts  1.57 us

profile of v7, /device:TPU:0, one launch (start us, length us, event | category | flops | bytes accessed | tf_op | source)
XLA Modules:
  0.0 34.6 jit_solution(7746651678082647486)
XLA Ops:
  0.0 33.1 %shard_map.73 = f32[8,32,128]{2,1,0:T(8,128)} custom-call(f32[8,64,256]{2,1,0:T(8,128)} %flux_h.1, f32[32,128]{1,0:T(8,128)} %diff_h.1, bf16[8,2,768,128]{3,2,1,0:T(8,128)(2,1)} %bitcast.5, s32[1,128]{1,0:T(1,128)} %bitcast.6, s32[1,128]{1,0:T(1,128)} %bitcast.7, s32[1,128]{1,0:T(1,128)} %bitcast.8, s32[1,128]{1,0:T(1,128)} %bitcast.9), custom_call_target="tpu_custom_call" | custom-call | tf_op jit(solution)/shard_map/pallas_call | solution.py:450
  33.1 1.6 %copy.9 = f32[8,32,128]{2,1,0:T(8,128)} copy(f32[8,32,128]{2,1,0:T(8,128)} %shard_map.73) | data formatting | bytes 262144

commit v8 on v7

--- a/solution.py
+++ b/solution.py
@@ -82,6 +82,7 @@
 
         lax.fori_loop(0, nx, one_row, 0)
 
+    pitch = rows + 8
     quarter = fields // 4
     flux_ins = [
         pltpu.make_async_copy(flux_h.at[pl.ds(i * quarter, quarter)], flux.at[pl.ds(i * quarter, quarter)], in_sem.at[5 + i])
@@ -117,7 +118,7 @@
         c.start()
     for f in range(fields):
         for h in range(2):
-            xs[0, h, f * rows : (f + 1) * rows, :] = flux[f, :, h * LANES : (h + 1) * LANES]
+            xs[0, h, f * pitch : f * pitch + rows, :] = flux[f, :, h * LANES : (h + 1) * LANES]
     lane_c = lane_of((rows, LANES))
     first = jnp.zeros((rows, LANES), jnp.float32)
     last = jnp.zeros((rows, LANES), jnp.float32)
@@ -129,8 +130,8 @@
     col_s[0] = first
     col_s[1] = last
     for h in range(2):
-        row_s[0, h] = xs[0, h, pl.ds(0, fields, stride=rows), :]
-        row_s[1, h] = xs[0, h, pl.ds(rows - 1, fields, stride=rows), :]
+        row_s[0, h] = xs[0, h, pl.ds(0, fields, stride=pitch), :]
+        row_s[1, h] = xs[0, h, pl.ds(rows - 1, fields, stride=pitch), :]
 
     pl.semaphore_wait(barrier, hn + beside_others)
 
@@ -222,7 +223,7 @@
                 parts = [
                     jnp.concatenate(
                         [
-                            xs[c, h, pl.ds(t * TILE_X + g * per + a, fields, stride=rows), :]
+                            xs[c, h, pl.ds(t * TILE_X + g * per + a, fields, stride=pitch), :]
                             for t in range(tiles_x)
                         ],
                         axis=0,
@@ -255,8 +256,8 @@
             x = halves[h]
             above = jnp.where(row_i == 0, row_r[0, h, f : f + 1, :], pltpu.roll(x, 1, 0))
             below = jnp.where(row_i == rows - 1, row_r[1, h, f : f + 1, :], pltpu.roll(x, rows - 1, 0))
-            xs[1, h, f * rows : (f + 1) * rows, :] = (below - above) * 0.5
-            xs[2, h, f * rows : (f + 1) * rows, :] = (after_y[h] - before_y[h]) * 0.5
+            xs[1, h, f * pitch : f * pitch + rows, :] = (below - above) * 0.5
+            xs[2, h, f * pitch : f * pitch + rows, :] = (after_y[h] - before_y[h]) * 0.5
 
     spread(1)
     spread(2)
@@ -458,7 +459,7 @@
             v((4, 1, records), jnp.int32),
             dma((9,)),
             v((nwb // 2, depth, 2 * LANES), bf16),
-            v((3, 2, (fields + 1) * rows, LANES), f32),
+            v((3, 2, (fields + 1) * (rows + 8), LANES), f32),
             v((tiles * fields, depth), bf16),
             v((nwb * tiles, fields, LANES), f32),
             v((n, LANES), jnp.int32),

time: 34.8 us -> 34.7 us (level)
  no operation moved by 1% of the time
where the time goes in v8:
time: 34.7 us; the launch traced here: 34.5 us
  Pallas kernels  32.9 us (95%)
  local copies, waits for them, and re-layouts  1.57 us (5%)
    pallas_call x1, Pallas kernels, local(): pl.pallas_call(functools.partial(kernel, nx, ny, cap), out_shape=jax.Shap...  32.9 us
    unnamed x1, local copies, waits for them, and re-layouts  1.57 us

profile of v8, /device:TPU:0, one launch (start us, length us, event | category | flops | bytes accessed | tf_op | source)
XLA Modules:
  0.0 34.5 jit_solution(12378698650290587008)
XLA Ops:
  0.0 32.9 %shard_map.73 = f32[8,32,128]{2,1,0:T(8,128)} custom-call(f32[8,64,256]{2,1,0:T(8,128)} %flux_h.1, f32[32,128]{1,0:T(8,128)} %diff_h.1, bf16[8,2,768,128]{3,2,1,0:T(8,128)(2,1)} %bitcast.5, s32[1,128]{1,0:T(1,128)} %bitcast.6, s32[1,128]{1,0:T(1,128)} %bitcast.7, s32[1,128]{1,0:T(1,128)} %bitcast.8, s32[1,128]{1,0:T(1,128)} %bitcast.9), custom_call_target="tpu_custom_call" | custom-call | tf_op jit(solution)/shard_map/pallas_call | solution.py:451
  32.9 1.6 %copy.9 = f32[8,32,128]{2,1,0:T(8,128)} copy(f32[8,32,128]{2,1,0:T(8,128)} %shard_map.73) | data formatting | bytes 262144

commit v9 on v8

--- a/solution.py
+++ b/solution.py
@@ -270,7 +270,7 @@
         prod[pl.ds((2 * p + 1) * tiles, tiles)] = got_pair[:, LANES:].reshape(tiles, fields, LANES)
         return c
 
-    lax.fori_loop(0, nwb // 2, products, 0)
+    lax.fori_loop(0, nwb // 2, products, 0, unroll=2)
     table_copy.wait()
 
     def record(d, s):

time: 34.7 us -> 34 us (0.980)
  Pallas kernels: 32.9 us -> 32.2 us
    pallas_call x1, Pallas kernels: 32.9 us -> 32.2 us  [local(): pl.pallas_call(functools.partial(kernel, nx, ny, cap), out_shape=jax.Shap...]
where the time goes in v9:
time: 34 us; the launch traced here: 33.8 us
  Pallas kernels  32.2 us (95%)
  local copies, waits for them, and re-layouts  1.57 us (5%)
    pallas_call x1, Pallas kernels, local(): pl.pallas_call(functools.partial(kernel, nx, ny, cap), out_shape=jax.Shap...  32.2 us
    unnamed x1, local copies, waits for them, and re-layouts  1.57 us

profile of v9, /device:TPU:0, one launch (start us, length us, event | category | flops | bytes accessed | tf_op | source)
XLA Modules:
  0.0 33.8 jit_solution(560358023007843712)
XLA Ops:
  0.0 32.2 %shard_map.73 = f32[8,32,128]{2,1,0:T(8,128)} custom-call(f32[8,64,256]{2,1,0:T(8,128)} %flux_h.1, f32[32,128]{1,0:T(8,128)} %diff_h.1, bf16[8,2,768,128]{3,2,1,0:T(8,128)(2,1)} %bitcast.5, s32[1,128]{1,0:T(1,128)} %bitcast.6, s32[1,128]{1,0:T(1,128)} %bitcast.7, s32[1,128]{1,0:T(1,128)} %bitcast.8, s32[1,128]{1,0:T(1,128)} %bitcast.9), custom_call_target="tpu_custom_call" | custom-call | tf_op jit(solution)/shard_map/pallas_call | solution.py:451
  32.2 1.6 %copy.9 = f32[8,32,128]{2,1,0:T(8,128)} copy(f32[8,32,128]{2,1,0:T(8,128)} %shard_map.73) | data formatting | bytes 262144
